TPU v7x, 128 devices: a whole 4x4x4 slice. The times are simulated.
128 devices in a mesh: row: 8 (over x_hi, z), col: 16 (over x_lo, y, core).
Axes of the slice: x: 4 (x_hi: 2, x_lo: 2; x = x_hi * 2 + x_lo), y: 4, z: 4, core: 2. Of those that a mesh axis runs over, the one named last changes fastest.
Arguments:
- pair_rep: float32 [384, 384, 128], P('row', 'col'), may hold values from -24 to 24
- chain_id: int32 [384], replicated, may hold values from 0 to 3, never falling along the last dimension, each value on 1 to 192 neighbouring positions
- live_mask: int32 [384], replicated, may hold values from 0 to 1, as said below
- chain_table: float32 [2, 128], replicated, may hold values from -4 to 4
- tri_proj: bfloat16 [2, 128, 512], replicated, may hold values from -0.5 to 0.5
- tri_gate: bfloat16 [2, 128, 128], replicated, may hold values from -0.5 to 0.5
- tri_out: bfloat16 [2, 128, 128], replicated, may hold values from -0.5 to 0.5
- att_project: bfloat16 [2, 128, 512], replicated, may hold values from -0.5 to 0.5
- att_bias: float32 [2, 128, 4], replicated, may hold values from -20 to 20
- att_out: bfloat16 [2, 128, 128], replicated, may hold values from -0.5 to 0.5
Outputs:
- pair_out: float32 [384, 384, 128], P('row', 'col')
Inputs may be any that keep to these rules, and one draw needn't show every extreme that they name: chain_id never falls along the residues, and each of the 4 chains holds at least one residue. live_mask is 1 on the first residues and 0 on the rest; at least 192 residues are live.
All inputs are finite; a program needn't handle non-finite values.
Results may differ from a plain program's by a relative error of at most 0.0075.
Values may be sent and summed in bfloat16 or wider, within the bound.
A program may use at most 128 MiB of HBM per device.

v0:
```python
import jax
import jax.numpy as jnp
from jax import lax
from jax.sharding import PartitionSpec as P

CZ = 128
CH = 128
HEADS = 4
DH = 32


def broadcast(block, axis, source):
    block = jnp.where(lax.axis_index(axis) == source, block, jnp.zeros_like(block))
    return lax.psum(block, axis)


def layer_norm(values):
    center = values - jnp.mean(values, axis=-1, keepdims=True)
    spread = jnp.mean(center * center, axis=-1, keepdims=True)
    return center / jnp.sqrt(spread + 1e-05)


def project_pair(pair_state, pair_mask, weights):
    rows_here, cols_here = (pair_state.shape[0], pair_state.shape[1])
    normed = layer_norm(pair_state).astype(jnp.bfloat16)
    flat_in = normed.reshape(rows_here * cols_here, CZ)
    projected = jnp.dot(flat_in, weights, preferred_element_type=jnp.float32).reshape(
        rows_here, cols_here, 4 * CH
    )
    masked = pair_mask[:, :, None]
    left_side = (
        masked * jax.nn.sigmoid(projected[:, :, CH : 2 * CH]) * projected[:, :, :CH]
    ).astype(jnp.bfloat16)
    right_side = (
        masked * jax.nn.sigmoid(projected[:, :, 3 * CH :]) * projected[:, :, 2 * CH : 3 * CH]
    ).astype(jnp.bfloat16)
    return (flat_in, left_side, right_side)


def finish_triangle(pair_state, flat_in, product, gate_weight, out_weight):
    mixed_norm = layer_norm(product).astype(jnp.bfloat16)
    gate_value = jax.nn.sigmoid(jnp.dot(flat_in, gate_weight, preferred_element_type=jnp.float32))
    update = gate_value * jnp.dot(
        mixed_norm.reshape(-1, CH), out_weight, preferred_element_type=jnp.float32
    )
    return pair_state + update.reshape(pair_state.shape)


def full_bias(normed, bias_weight, row_count, col_count):
    rows_here, cols_here = (normed.shape[0], normed.shape[1])
    tile_bias = jnp.dot(
        normed.reshape(rows_here * cols_here, CZ),
        bias_weight,
        precision=lax.Precision.HIGHEST,
        preferred_element_type=jnp.float32,
    )
    tile_bias = jnp.transpose(tile_bias.reshape(rows_here, cols_here, HEADS), (2, 0, 1))
    gathered = lax.all_gather(tile_bias, ("row", "col"), axis=0, tiled=True)
    gathered = gathered.reshape(row_count, col_count, HEADS, rows_here, cols_here)
    gathered = jnp.transpose(gathered, (2, 0, 3, 1, 4))
    return gathered.reshape(HEADS, row_count * rows_here, col_count * cols_here)


def attend_heads(query_all, keys_all, values_all, pair_bias, key_bias, flipped):
    scaling = DH ** (-0.5)

    def one_head(inputs):
        query_head, keys_head, values_head, bias_head = inputs
        if flipped:
            bias_head = bias_head.T
        scores = (
            jnp.einsum("ijd,ikd->ijk", query_head, keys_head, preferred_element_type=jnp.float32)
            * scaling
            + bias_head[None]
            + key_bias
        )
        scores = scores - jnp.max(scores, axis=-1, keepdims=True)
        exponent = jnp.exp(scores)
        weight = (exponent / jnp.sum(exponent, axis=-1, keepdims=True)).astype(jnp.bfloat16)
        return jnp.einsum("ijk,ikd->ijd", weight, values_head, preferred_element_type=jnp.float32)

    return lax.map(one_head, (query_all, keys_all, values_all, pair_bias))


def line_update(line_rows, pair_bias, key_bias, weights, out_weight, flipped):
    first_dim, second_dim = (line_rows.shape[0], line_rows.shape[1])
    projected = jnp.dot(
        line_rows.reshape(first_dim * second_dim, CZ), weights, preferred_element_type=jnp.float32
    )
    projected = projected.reshape(first_dim, second_dim, 4, HEADS, DH)
    rounded = projected[:, :, :3].astype(jnp.bfloat16)
    axes_order = (2, 3, 1, 0, 4) if flipped else (2, 3, 0, 1, 4)
    heads_first = jnp.transpose(rounded, axes_order)
    attended = attend_heads(
        heads_first[0], heads_first[1], heads_first[2], pair_bias, key_bias, flipped
    )
    back_order = (2, 1, 0, 3) if flipped else (1, 2, 0, 3)
    attended = jnp.transpose(attended, back_order)
    gate_value = jax.nn.sigmoid(projected[:, :, 3])
    gated = (gate_value * attended).astype(jnp.bfloat16).reshape(first_dim * second_dim, CZ)
    update = jnp.dot(gated, out_weight, preferred_element_type=jnp.float32).astype(jnp.bfloat16)
    return update.reshape(first_dim, second_dim, CZ)


def local(
    pair_rep,
    chain_id,
    live_mask,
    chain_table,
    tri_proj,
    tri_gate,
    tri_out,
    att_project,
    att_bias,
    att_out,
):
    rows_here, cols_here = (pair_rep.shape[0], pair_rep.shape[1])
    row_count = lax.axis_size("row")
    col_count = lax.axis_size("col")
    panel_count = col_count // row_count
    row_index = lax.axis_index("row")
    col_index = lax.axis_index("col")
    chain_rows = lax.dynamic_slice_in_dim(chain_id, row_index * rows_here, rows_here)
    chain_cols = lax.dynamic_slice_in_dim(chain_id, col_index * cols_here, cols_here)
    live_float = live_mask.astype(jnp.float32)
    live_rows = lax.dynamic_slice_in_dim(live_float, row_index * rows_here, rows_here)
    live_cols = lax.dynamic_slice_in_dim(live_float, col_index * cols_here, cols_here)
    same_chain = chain_rows[:, None] == chain_cols[None, :]
    pair_state = pair_rep + jnp.where(same_chain[:, :, None], chain_table[1], chain_table[0])
    pair_mask = live_rows[:, None] * live_cols[None, :]
    key_bias = (live_float - 1.0) * 1000000000.0
    flat_in, left_side, right_side = project_pair(pair_state, pair_mask, tri_proj[0])
    left_rows, right_rows = (
        lax.all_gather(left_side, "col", axis=1, tiled=True),
        lax.all_gather(right_side, "col", axis=1, tiled=True),
    )
    portion = col_index % panel_count
    row_block = lax.dynamic_slice_in_dim(right_rows, portion * cols_here, cols_here, 0)
    right_cols = broadcast(row_block, "row", col_index // panel_count)
    product = jnp.einsum("ikc,jkc->ijc", left_rows, right_cols, preferred_element_type=jnp.float32)
    pair_state = finish_triangle(pair_state, flat_in, product, tri_gate[0], tri_out[0])
    flat_in, left_side, right_side = project_pair(pair_state, pair_mask, tri_proj[1])
    left_strip, right_strip = (
        lax.all_gather(left_side, "row", axis=0, tiled=True),
        lax.all_gather(right_side, "row", axis=0, tiled=True),
    )
    blocks = []
    for portion in range(panel_count):
        panel_now = broadcast(left_strip, "col", row_index * panel_count + portion)
        blocks.append(
            jnp.einsum("kic,kjc->ijc", panel_now, right_strip, preferred_element_type=jnp.float32)
        )
    product = jnp.concatenate(blocks, axis=0)
    pair_state = finish_triangle(pair_state, flat_in, product, tri_gate[1], tri_out[1])
    normed = layer_norm(pair_state)
    pair_bias = full_bias(normed, att_bias[0], row_count, col_count)
    line_rows = lax.all_to_all(
        normed.astype(jnp.bfloat16), "col", split_axis=0, concat_axis=1, tiled=True
    )
    update = line_update(line_rows, pair_bias, key_bias, att_project[0], att_out[0], False)
    returned = lax.all_to_all(update, "col", split_axis=1, concat_axis=0, tiled=True)
    pair_state = pair_state + returned.astype(jnp.float32)
    normed = layer_norm(pair_state)
    pair_bias = full_bias(normed, att_bias[1], row_count, col_count)
    line_cols = lax.all_to_all(
        normed.astype(jnp.bfloat16), "row", split_axis=1, concat_axis=0, tiled=True
    )
    update = line_update(line_cols, pair_bias, key_bias, att_project[1], att_out[1], True)
    returned = lax.all_to_all(update, "row", split_axis=0, concat_axis=1, tiled=True)
    pair_state = pair_state + returned.astype(jnp.float32)
    return pair_state


def solution(mesh):
    return jax.shard_map(
        local,
        mesh=mesh,
        in_specs=(P("row", "col", None), P(), P(), P(), P(), P(), P(), P(), P(), P()),
        out_specs=P("row", "col", None),
        check_vma=False,
    )
```

profile of v0, /device:TPU:0, one launch (start us, length us, event | category | flops | bytes accessed | tf_op | source)
XLA Modules:
  0.0 985.3 jit_solution(2209195052078152962)
XLA Ops:
  9.8 1.5 fusion.115
  11.3 1.6 multiply_reduce_fusion.5
  14.1 1.2 fusion.102
  16.2 40.4 %all-gather.7.cloned.1.call-done = bf16[48,384,128]{2,1,0:T(8,128)(2,1)} async-done(((bf16[48,24,128]{2,1,0:T(8,128)(2,1)}), bf16[48,384,128]{2,1,0:T(8,128)(2,1)}) %all-gather.7.cloned.1.call-update) | async-done | bytes 4718608 | tf_op jit(solution)/shard_map/all_gather | solution.py:135
  56.6 3.3 dynamic-slice_select_fusion
  61.0 36.0 %all-gather.9.cloned.1.call-done = bf16[48,384,128]{2,1,0:T(8,128)(2,1)} async-done(((bf16[48,24,128]{2,1,0:T(8,128)(2,1)}), bf16[48,384,128]{2,1,0:T(8,128)(2,1)}) %all-gather.9.cloned.1.call-update) | async-done | bytes 4718608 | tf_op jit(solution)/shard_map/all_gather | solution.py:134
  97.0 22.1 %copy.200 = bf16[48,384,128]{0,1,2:T(8,128)(2,1)} copy(bf16[48,384,128]{2,1,0:T(8,128)(2,1)} %all-gather.9.cloned.1.call-done) | data formatting | bytes 9437184 | tf_op jit(solution)/shard_map/all_gather | solution.py:134
  119.2 75.3 %all-reduce.4.cloned.1.call-done = bf16[24,384,128]{2,1,0:T(8,128)(2,1)} async-done(((bf16[24,384,128]{2,1,0:T(8,128)(2,1)}), bf16[24,384,128]{2,1,0:T(8,128)(2,1)}) %all-reduce.4.cloned.1.call-update) | async-done | bytes 2359312 | tf_op jit(solution)/shard_map/psum | solution.py:14
  194.5 4.5 copy.199
  199.0 7.6 bitcast_reduce_fusion
  208.0 0.9 divide_convert_fusion.4
  209.5 1.0 convolution_multiply_fusion.1
  212.2 1.2 fusion.92
  214.0 54.4 %all-gather.13.cloned.1.call-done = bf16[384,24,128]{2,1,0:T(8,128)(2,1)} async-done(((bf16[48,24,128]{2,1,0:T(8,128)(2,1)}), bf16[384,24,128]{2,1,0:T(8,128)(2,1)}) %all-gather.13.cloned.1.call-update) | async-done | bytes 2359312 | tf_op jit(solution)/shard_map/all_gather | solution.py:144
  268.4 3.7 copy.206
  272.1 2.6 broadcast_select_fusion.1
  275.6 1.1 fusion.76
  276.8 48.0 %all-gather.11.cloned.1.call-done = bf16[384,24,128]{2,1,0:T(8,128)(2,1)} async-done(((bf16[48,24,128]{2,1,0:T(8,128)(2,1)}), bf16[384,24,128]{2,1,0:T(8,128)(2,1)}) %all-gather.11.cloned.1.call-update) | async-done | bytes 2359312 | tf_op jit(solution)/shard_map/all_gather | solution.py:145
  324.8 3.7 copy.207
  328.5 127.9 %all-reduce.6.cloned.1.call-done = (bf16[384,24,128]{0,1,2:T(8,128)(2,1)}, bf16[384,24,128]{0,1,2:T(8,128)(2,1)}) async-done(((bf16[384,24,128]{0,1,2:T(8,128)(2,1)}, bf16[384,24,128]{0,1,2:T(8,128)(2,1)}), (bf16[384,24,128]{0,1,2:T(8,128)(2,1)}, bf16[384,24,128]{0,1,2:T(8,128)(2,1)})) %all-reduce.6.cloned.1.call-update) | async-done | bytes 4718608 | tf_op jit(solution)/shard_map/psum | solution.py:14
  456.4 3.9 convolution_bitcast_fusion.3
  460.3 1.9 copy.210
  462.2 3.9 convolution_bitcast_fusion.2
  466.1 1.9 copy.211
  470.0 3.1 convolution_bitcast_fusion.5
  473.8 1.1 fusion.117
  474.9 4.6 all-to-all-start
  480.6 7.4 all-to-all-done
  488.6 1.4 copy-done.4
  490.1 1.0 slice_bitcast_fusion.3
  491.1 185.0 %all-gather.15.cloned.1.call-done = f32[512,48,24]{1,2,0:T(8,128)} async-done(((f32[4,48,24]{1,2,0:T(8,128)}), f32[512,48,24]{1,2,0:T(8,128)}) %all-gather.15.cloned.1.call-update) | async-done | bytes 2359312 | tf_op jit(solution)/shard_map/all_gather | solution.py:58
  676.0 9.1 copy.215
  685.1 4.8 reshape.283
  690.8 17.2 %while.20 = (s32[]{:T(128)}, f32[4,3,384,32]{2,3,0,1:T(8,128)}, bf16[4,3,384,32]{2,3,0,1:T(8,128)(2,1)}, bf16[4,3,384,32]{2,3,0,1:T(8,128)(2,1)}, f32[4,384,384]...) while((s32[]{:T(128)}, f32[4,3,384,32]{2,3,0,1:T(8,128)}, ...), condition=%wide.region_16.17_spmd, body=%wide.region_13.16_spmd.sunk | while | flops 89802624 | bytes 2890841 | solution.py:82
  690.8 1.7 fusion.194
  692.5 2.6 fusion.195
  695.1 1.7 fusion.194
  696.8 2.6 fusion.195
  699.4 1.7 fusion.194
  701.1 2.6 fusion.195
  703.7 1.7 fusion.194
  705.4 2.5 fusion.195
  708.0 1.4 fusion.112
  710.3 13.0 %all_to_all.48 = bf16[3,384,128]{2,0,1:T(4,128)(2,1)S(1)} all-to-all(bf16[3,384,128]{2,0,1:T(4,128)(2,1)S(1)} %copy.221), channel_id=1, replica_groups=mesh['row'=8,'col'=16] {'col'}, dimensions={1} | all-to-all | bytes 589824 | tf_op jit(solution)/shard_map/all_to_all | solution.py:161
  724.1 3.1 convolution_bitcast_fusion.4
  729.1 5.0 all-to-all-start.2
  734.3 8.9 all-to-all-done.2
  743.7 1.4 copy-done.3
  745.2 1.0 slice_bitcast_fusion
  746.2 180.6 %all-gather.17.cloned.1.call-done = f32[512,48,24]{1,2,0:T(8,128)} async-done(((f32[4,48,24]{1,2,0:T(8,128)}), f32[512,48,24]{1,2,0:T(8,128)}) %all-gather.17.cloned.1.call-update) | async-done | bytes 2359312 | tf_op jit(solution)/shard_map/all_gather | solution.py:58
  926.8 9.1 copy.267
  935.9 4.8 reshape.287
  941.5 18.1 %while.21 = (s32[]{:T(128)}, f32[4,3,384,32]{2,3,0,1:T(8,128)}, bf16[4,3,384,32]{2,3,0,1:T(8,128)(2,1)}, bf16[4,3,384,32]{2,3,0,1:T(8,128)(2,1)}, f32[4,384,384]...) while((s32[]{:T(128)}, f32[4,3,384,32]{2,3,0,1:T(8,128)}, ...), condition=%wide.region_22.23_spmd, body=%wide.region_19.22_spmd.sunk | while | flops 89802624 | bytes 4070489 | solution.py:82
  941.8 1.7 fusion.201
  943.5 2.5 fusion.202
  946.3 1.7 fusion.201
  948.0 2.5 fusion.202
  950.9 1.7 fusion.201
  952.6 2.5 fusion.202
  955.4 1.7 fusion.201
  957.1 2.6 fusion.202
  959.7 1.4 fusion.113
  962.8 14.4 %all_to_all.49 = bf16[384,3,128]{2,1,0:T(4,128)(2,1)S(1)} all-to-all(bf16[384,3,128]{2,1,0:T(4,128)(2,1)S(1)} %reshape.289), channel_id=1, replica_groups=mesh['row'=8,'col'=16] {'row'}, dimensions={0} | all-to-all | bytes 589824 | tf_op jit(solution)/shard_map/all_to_all | solution.py:169
  977.3 1.0 copy_add_fusion
  (135 shorter events, 24.7 us)
Async XLA Ops:
  6.5 6.4 copy-start.2
  6.5 7.0 copy-start.7
  6.5 50.0 %all-gather.7.cloned.1.call-start = ((), (), s32[]{:S(2)}) async-start(), calls=%async_computation.4 | async-start | bytes 5013504 | tf_op jit(solution)/shard_map/all_gather | solution.py:135
  14.1 2.0 copy-start.10
  15.3 81.7 %all-gather.9.cloned.1.call-start = ((), (), s32[]{:S(2)}) async-start(), calls=%async_computation.6 | async-start | bytes 5013504 | tf_op jit(solution)/shard_map/all_gather | solution.py:134
  16.1 178.4 %all-reduce.4.cloned.1.call-start = ((), (), s32[]{:S(2)}) async-start(), calls=%async_computation.5 | async-start | bytes 4718592 | tf_op jit(solution)/shard_map/psum | solution.py:14
  59.8 0.8 copy-start.17
  59.9 208.6 %all-gather.13.cloned.1.call-start = ((), (), s32[]{:S(2)}) async-start(), calls=%async_computation.8 | async-start | bytes 2654208 | tf_op jit(solution)/shard_map/all_gather | solution.py:144
  206.7 0.6 copy-start.12
  210.5 1.2 copy-start.8
  211.3 0.9 copy-start.11
  213.4 111.4 %all-gather.11.cloned.1.call-start = ((), (), s32[]{:S(2)}) async-start(), calls=%async_computation.7 | async-start | bytes 2654208 | tf_op jit(solution)/shard_map/all_gather | solution.py:145
  214.0 242.4 %all-reduce.6.cloned.1.call-start = ((), (), s32[]{:S(2)}) async-start(), calls=%async_computation.11 | async-start | bytes 9437184 | tf_op jit(solution)/shard_map/psum | solution.py:14
  274.8 0.8 copy-start.18
  274.8 401.2 %all-gather.15.cloned.1.call-start = ((), (), s32[]{:S(2)}) async-start(), calls=%async_computation.9 | async-start | bytes 6340608 | tf_op jit(solution)/shard_map/all_gather | solution.py:58
  466.1 3.0 copy-start.5
  466.1 3.0 copy-start.13
  469.1 0.9 copy-start.19
  470.0 9.8 copy-start.9
  473.1 7.5 copy-start.16
  474.9 13.1 %all-to-all-start = ((bf16[48,24,128]{2,1,0:T(8,128)(2,1)}), bf16[48,24,128]{2,1,0:T(8,128)(2,1)S(1)}, u32[]{:S(2)}, u32[]{:S(2)}) async-start(bf16[48,24,128]{2,1,0:T(8,128)(2,1)} %fusion.117), calls=%async_computation | async-start | bytes 589824 | tf_op jit(solution)/shard_map/all_to_all | solution.py:157
  479.6 447.2 %all-gather.17.cloned.1.call-start = ((), (), s32[]{:S(2)}) async-start(), calls=%async_computation.10 | async-start | bytes 6340608 | tf_op jit(solution)/shard_map/all_gather | solution.py:58
  488.5 1.4 copy-start.4
  708.0 1.8 copy-start.14
  723.7 4.7 copy-start
  724.1 10.0 %copy-start.6 = (bf16[512,128]{0,1:T(8,128)(2,1)S(1)}, bf16[512,128]{0,1:T(8,128)(2,1)}, u32[]{:S(2)}) copy-start(bf16[512,128]{0,1:T(8,128)(2,1)} %get-tuple-element.213) | copy-start | bytes 393220
  729.1 14.1 %all-to-all-start.2 = ((bf16[48,24,128]{2,0,1:T(8,128)(2,1)}), bf16[48,24,128]{2,0,1:T(8,128)(2,1)S(1)}, u32[]{:S(2)}, u32[]{:S(2)}) async-start(bf16[48,24,128]{2,0,1:T(8,128)(2,1)} %copy.224), calls=%async_computation.2 | async-start | bytes 589824 | tf_op jit(solution)/shard_map/all_to_all | solution.py:165
  743.7 1.4 copy-start.3
  961.1 1.4 copy-start.15
  962.5 14.8 %copy-start.1 = (f32[48,24,128]{2,1,0:T(8,128)S(1)}, f32[48,24,128]{2,1,0:T(8,128)}, u32[]{:S(2)}) copy-start(f32[48,24,128]{2,1,0:T(8,128)} %copy-done) | copy-start | bytes 1769476
Sparse Core Ops, SparseCore 0:
  15.4 41.0 all-gather.6
  58.2 38.7 all-gather.8
  99.6 94.8 all-reduce.3
  213.5 54.9 all-gather.12
  270.6 54.1 all-gather.10
  327.2 129.1 all-reduce.5
  474.0 202.0 all-gather.14
  728.1 198.6 all-gather.16
where the time goes:
time: 995 us; the launch traced here: 985 us
  waiting for transfers between devices  765 us (77%)
  local copies, waits for them, and re-layouts  84.1 us (8%)
  matrix products  60.6 us (6%)
  blocking collectives  27.4 us (3%)
  other arithmetic  22.8 us (2%)
  between operations  14.4 us (1%)
  starting transfers between devices  10.6 us (1%)
    all_gather x2, waiting for transfers between devices, full_bias(): gathered = lax.all_gather(tile_bias, ('row', 'col'), axis=0, tiled=True)  366 us
    psum x2, waiting for transfers between devices, broadcast(): return lax.psum(block, axis)  203 us
    all_gather x1, waiting for transfers between devices, local(): lax.all_gather(left_side, 'row', axis=0, tiled=True)  54.4 us
    all_gather x1, waiting for transfers between devices, local(): lax.all_gather(right_side, 'row', axis=0, tiled=True)  48 us
    all_gather x1, waiting for transfers between devices, local(): lax.all_gather(right_side, 'col', axis=1, tiled=True)  40.4 us
    all_gather x1, waiting for transfers between devices, local(): lax.all_gather(left_side, 'col', axis=1, tiled=True)  36 us
    all_gather x1, local copies, waits for them, and re-layouts, local(): lax.all_gather(left_side, 'col', axis=1, tiled=True)  22.1 us
    dot_general x8, matrix products, one_head(): jnp.einsum('ijk,ikd->ijd', weight, values_head, preferred_element_type=jn...  20.4 us
  transfers between devices with their start and end apart: 10, of which 10 were waited for; matrix products, arithmetic and copies ran while one was open for 4% of the time, Pallas kernels for 0%

commit v1 on v0

--- a/solution.py
+++ b/solution.py
@@ -1,49 +1,197 @@
+import functools
 import jax
 import jax.numpy as jnp
 from jax import lax
 from jax.sharding import PartitionSpec as P
-
+from jax.experimental import pallas as pl
+from jax.experimental.pallas import tpu as pltpu
+
+F32 = jnp.float32
+BF16 = jnp.bfloat16
+MESH = pl.DeviceIdType.MESH
 CZ = 128
-CH = 128
+ROWS, COLS = 8, 16
+IL, JL = 48, 24
+PX = IL * JL
+NRES = 384
+NDEV = ROWS * COLS
+QS = PX // 128
+GO, BACK = 32, 16
+GO32, BACK32 = 24, 16
+
+
+def normalize(v):
+    mean = jnp.mean(v, axis=-1, keepdims=True)
+    c = v - mean
+    spread = jnp.mean(c * c, axis=-1, keepdims=True)
+    return c * lax.rsqrt(spread + 1e-05)
+
+
+def dot(a, b, dims=((1,), (0,))):
+    return lax.dot_general(a, b, (dims, ((), ())), preferred_element_type=F32)
+
+
+def exchange_start(src, dst, send, recv, r, s):
+    me = r * COLS + s
+
+    def go(d, _):
+        p = jnp.bitwise_xor(me, d)
+        pltpu.make_async_remote_copy(
+            src_ref=src.at[p], dst_ref=dst.at[me], send_sem=send, recv_sem=recv,
+            device_id=(p // COLS, p % COLS), device_id_type=MESH,
+        ).start()
+        return 0
+
+    lax.fori_loop(1, NDEV, go, 0)
+    dst[me] = src[me]
+
+
+def exchange_wait(src, dst, send, recv):
+    part = pl.ds(0, NDEV - 1)
+    pltpu.make_async_copy(src.at[part], dst.at[part], recv).wait()
+    pltpu.make_async_copy(src.at[part], dst.at[part], send).wait()
+
+
+def triangle(t, x, mask, proj, gate, out, nb, stage, send_go, recv_go, send_back, recv_back, left, right, sems, r, s, before_send):
+    def side(q, _):
+        rows = pl.ds(pl.multiple_of(q * 128, 128), 128)
+        n = normalize(x[rows, :]).astype(BF16)
+        nb[rows, :] = n
+        p = dot(n, proj[t])
+        m = mask[pl.ds(q, 1), :]
+        for k in range(2):
+            v = jax.nn.sigmoid(p[:, (2 * k + 1) * CZ:(2 * k + 2) * CZ]) * p[:, 2 * k * CZ:(2 * k + 1) * CZ]
+            stage[pl.ds(k * QS + q, CZ, stride=GO32), :] = v.T * m
+        return 0
+
+    lax.fori_loop(0, QS, side, 0)
+
+    def pack(c, _):
+        f = stage[pl.ds(pl.multiple_of(c * GO32, GO32), GO32), :]
+        send_go[c] = jnp.concatenate([f, jnp.zeros((GO - GO32, 128), F32)], axis=0).astype(BF16)
+        return 0
+
+    lax.fori_loop(0, CZ, pack, 0, unroll=4)
+    before_send()
+    exchange_start(send_go, recv_go, sems.at[0], sems.at[1], r, s)
+    exchange_wait(send_go, recv_go, sems.at[0], sems.at[1])
+
+    def unpack(c, _):
+        stage[pl.ds(pl.multiple_of(c * GO32, GO32), GO32), :] = recv_go[c].astype(F32)[:GO32]
+        return 0
+
+    lax.fori_loop(0, NDEV, unpack, 0, unroll=4)
+
+    for k, ref in enumerate((left, right)):
+        def gather(a, _):
+            v = []
+            for rr in range(ROWS):
+                v.append(jnp.concatenate(
+                    [stage[pl.ds(rr * COLS * GO32 + k * QS + 3 * a + i, COLS, stride=GO32), :] for i in range(3)], axis=1))
+            for b in range(8):
+                row = jnp.concatenate([u[:, IL * b:IL * (b + 1)] for u in v], axis=1)
+                for i in range(3):
+                    ref[pl.ds(i * NRES + 8 * a + b, COLS, stride=JL), :] = row[:, 128 * i:128 * (i + 1)]
+            return 0
+
+        lax.fori_loop(0, 3, gather, 0)
+    lf = jnp.concatenate([left[pl.ds(i * NRES, NRES), :] for i in range(3)], axis=1).astype(BF16)
+    rt = jnp.concatenate([right[pl.ds(i * NRES, NRES), :] for i in range(3)], axis=1).astype(BF16)
+    prod = dot(rt, lf, ((0,), (0,))) if t == 0 else dot(rt, lf, ((1,), (1,)))
+    for i in range(3):
+        left[pl.ds(i * NRES, NRES), :] = prod[:, 128 * i:128 * (i + 1)]
+
+    def scatter(a, _):
+        v = []
+        for b in range(8):
+            v.append(jnp.concatenate([left[pl.ds(i * NRES + 8 * a + b, COLS, stride=JL), :] for i in range(3)], axis=1))
+        for rr in range(ROWS):
+            row = jnp.concatenate([u[:, IL * rr:IL * (rr + 1)] for u in v], axis=1)
+            for i in range(3):
+                stage[pl.ds(rr * COLS * BACK32 + 3 * a + i, COLS, stride=BACK32), :] = row[:, 128 * i:128 * (i + 1)]
+        return 0
+
+    lax.fori_loop(0, 3, scatter, 0)
+
+    def pack2(c, _):
+        send_back[c] = stage[pl.ds(pl.multiple_of(c * BACK32, BACK32), BACK32), :].astype(BF16)
+        return 0
+
+    lax.fori_loop(0, NDEV, pack2, 0, unroll=4)
+    exchange_start(send_back, recv_back, sems.at[2], sems.at[3], r, s)
+    exchange_wait(send_back, recv_back, sems.at[2], sems.at[3])
+
+    def unpack2(c, _):
+        stage[pl.ds(pl.multiple_of(c * BACK32, BACK32), BACK32), :] = recv_back[c].astype(F32)
+        return 0
+
+    lax.fori_loop(0, CZ, unpack2, 0, unroll=4)
+
+    def finish(q, _):
+        rows = pl.ds(pl.multiple_of(q * 128, 128), 128)
+        pr = stage[pl.ds(q, CZ, stride=BACK32), :].T
+        mixed = normalize(pr).astype(BF16)
+        g = jax.nn.sigmoid(dot(nb[rows, :], gate[t]))
+        x[rows, :] = x[rows, :] + g * dot(mixed, out[t])
+        return 0
+
+    lax.fori_loop(0, QS, finish, 0)
+
+
+def tri_kernel(pair, mask, same, table, proj, gate, out, y, x, nb, stage, sg0, rg0, sb0, rb0, sg1, rg1, sb1, rb1, left, right, sems):
+    r = lax.axis_index("row")
+    s = lax.axis_index("col")
+    me = r * COLS + s
+    barrier = pltpu.get_barrier_semaphore()
+
+    def greet(d, _):
+        p = jnp.bitwise_xor(me, d)
+        pl.semaphore_signal(barrier, inc=1, device_id=(p // COLS, p % COLS), device_id_type=MESH)
+        return 0
+
+    lax.fori_loop(1, NDEV, greet, 0)
+    stage[...] = jnp.zeros_like(stage)
+    for j in range(JL):
+        part = pl.ds(j * IL, IL)
+        x[part, :] = pair[pl.ds(j, IL, stride=JL), :] + jnp.where(same[part, :] > 0, table[1:2, :], table[0:1, :])
+    triangle(0, x, mask, proj, gate, out, nb, stage, sg0, rg0, sb0, rb0, left, right, sems.at[0], r, s,
+             lambda: pl.semaphore_wait(barrier, NDEV - 1))
+    triangle(1, x, mask, proj, gate, out, nb, stage, sg1, rg1, sb1, rb1, left, right, sems.at[1], r, s, lambda: None)
+    for j in range(JL):
+        y[pl.ds(j, IL, stride=JL), :] = x[pl.ds(j * IL, IL), :]
+
+
+def tri_call(pair, mask, same, table, proj, gate, out):
+    vm = pl.BlockSpec(memory_space=pltpu.VMEM)
+    bufs = []
+    for _ in range(2):
+        bufs += [pltpu.VMEM((NDEV, GO, 128), BF16)] * 2 + [pltpu.VMEM((NDEV, BACK, 128), BF16)] * 2
+    return pl.pallas_call(
+        tri_kernel,
+        out_shape=jax.ShapeDtypeStruct((PX, CZ), F32),
+        in_specs=[vm] * 7,
+        out_specs=vm,
+        scratch_shapes=[
+            pltpu.VMEM((PX, CZ), F32),
+            pltpu.VMEM((PX, CZ), BF16),
+            pltpu.VMEM((NDEV * GO32, 128), F32),
+            *bufs,
+            pltpu.VMEM((3 * NRES, 128), F32),
+            pltpu.VMEM((3 * NRES, 128), F32),
+            pltpu.SemaphoreType.DMA((2, 4)),
+        ],
+        compiler_params=pltpu.CompilerParams(collective_id=0, has_side_effects=True, vmem_limit_bytes=48 << 20),
+    )(pair, mask, same, table, proj, gate, out)
+
+
 HEADS = 4
 DH = 32
-
-
-def broadcast(block, axis, source):
-    block = jnp.where(lax.axis_index(axis) == source, block, jnp.zeros_like(block))
-    return lax.psum(block, axis)
 
 
 def layer_norm(values):
     center = values - jnp.mean(values, axis=-1, keepdims=True)
     spread = jnp.mean(center * center, axis=-1, keepdims=True)
     return center / jnp.sqrt(spread + 1e-05)
-
-
-def project_pair(pair_state, pair_mask, weights):
-    rows_here, cols_here = (pair_state.shape[0], pair_state.shape[1])
-    normed = layer_norm(pair_state).astype(jnp.bfloat16)
-    flat_in = normed.reshape(rows_here * cols_here, CZ)
-    projected = jnp.dot(flat_in, weights, preferred_element_type=jnp.float32).reshape(
-        rows_here, cols_here, 4 * CH
-    )
-    masked = pair_mask[:, :, None]
-    left_side = (
-        masked * jax.nn.sigmoid(projected[:, :, CH : 2 * CH]) * projected[:, :, :CH]
-    ).astype(jnp.bfloat16)
-    right_side = (
-        masked * jax.nn.sigmoid(projected[:, :, 3 * CH :]) * projected[:, :, 2 * CH : 3 * CH]
-    ).astype(jnp.bfloat16)
-    return (flat_in, left_side, right_side)
-
-
-def finish_triangle(pair_state, flat_in, product, gate_weight, out_weight):
-    mixed_norm = layer_norm(product).astype(jnp.bfloat16)
-    gate_value = jax.nn.sigmoid(jnp.dot(flat_in, gate_weight, preferred_element_type=jnp.float32))
-    update = gate_value * jnp.dot(
-        mixed_norm.reshape(-1, CH), out_weight, preferred_element_type=jnp.float32
-    )
-    return pair_state + update.reshape(pair_state.shape)
 
 
 def full_bias(normed, bias_weight, row_count, col_count):
@@ -117,7 +265,6 @@
     rows_here, cols_here = (pair_rep.shape[0], pair_rep.shape[1])
     row_count = lax.axis_size("row")
     col_count = lax.axis_size("col")
-    panel_count = col_count // row_count
     row_index = lax.axis_index("row")
     col_index = lax.axis_index("col")
     chain_rows = lax.dynamic_slice_in_dim(chain_id, row_index * rows_here, rows_here)
@@ -126,32 +273,12 @@
     live_rows = lax.dynamic_slice_in_dim(live_float, row_index * rows_here, rows_here)
     live_cols = lax.dynamic_slice_in_dim(live_float, col_index * cols_here, cols_here)
     same_chain = chain_rows[:, None] == chain_cols[None, :]
-    pair_state = pair_rep + jnp.where(same_chain[:, :, None], chain_table[1], chain_table[0])
-    pair_mask = live_rows[:, None] * live_cols[None, :]
+    mask = (live_cols[:, None] * live_rows[None, :]).reshape(QS, 128)
+    same = jnp.broadcast_to(same_chain.T.reshape(PX, 1), (PX, CZ)).astype(jnp.int32)
     key_bias = (live_float - 1.0) * 1000000000.0
-    flat_in, left_side, right_side = project_pair(pair_state, pair_mask, tri_proj[0])
-    left_rows, right_rows = (
-        lax.all_gather(left_side, "col", axis=1, tiled=True),
-        lax.all_gather(right_side, "col", axis=1, tiled=True),
-    )
-    portion = col_index % panel_count
-    row_block = lax.dynamic_slice_in_dim(right_rows, portion * cols_here, cols_here, 0)
-    right_cols = broadcast(row_block, "row", col_index // panel_count)
-    product = jnp.einsum("ikc,jkc->ijc", left_rows, right_cols, preferred_element_type=jnp.float32)
-    pair_state = finish_triangle(pair_state, flat_in, product, tri_gate[0], tri_out[0])
-    flat_in, left_side, right_side = project_pair(pair_state, pair_mask, tri_proj[1])
-    left_strip, right_strip = (
-        lax.all_gather(left_side, "row", axis=0, tiled=True),
-        lax.all_gather(right_side, "row", axis=0, tiled=True),
-    )
-    blocks = []
-    for portion in range(panel_count):
-        panel_now = broadcast(left_strip, "col", row_index * panel_count + portion)
-        blocks.append(
-            jnp.einsum("kic,kjc->ijc", panel_now, right_strip, preferred_element_type=jnp.float32)
-        )
-    product = jnp.concatenate(blocks, axis=0)
-    pair_state = finish_triangle(pair_state, flat_in, product, tri_gate[1], tri_out[1])
+    pair_state = tri_call(
+        pair_rep.reshape(PX, CZ), mask, same, chain_table, tri_proj, tri_gate, tri_out
+    ).reshape(rows_here, cols_here, CZ)
     normed = layer_norm(pair_state)
     pair_bias = full_bias(normed, att_bias[0], row_count, col_count)
     line_rows = lax.all_to_all(

time: 995 us -> 615 us (0.62)
  waiting for transfers between devices: 765 us -> 380 us
  Pallas kernels: 0 us -> 85 us
  local copies, waits for them, and re-layouts: 84.1 us -> 52.1 us
  matrix products: 60.6 us -> 38.3 us
  other arithmetic: 22.8 us -> 8.13 us
    psum x2 -> x0, waiting for transfers between devices: 203 us -> none  [broadcast(): return lax.psum(block, axis)]
    all_gather x4 -> x0, waiting for transfers between devices: 179 us -> none  [the longest x1 54.4 us: local(): lax.all_gather(left_side, 'row', axis=0, tiled=True)]
    pallas_call x0 -> x1, Pallas kernels: none -> 85 us  [tri_call(): pl.pallas_call(tri_kernel, out_shape=jax.ShapeDtypeStruct((PX, CZ), F32),...]
    all_gather x3 -> x0, local copies, waits for them, and re-layouts: 29.6 us -> none  [the longest x1 22.1 us: local(): lax.all_gather(left_side, 'col', axis=1, tiled=True)]
    dot_general x9 -> x0, matrix products: 19 us -> none  [the longest x2 7.84 us: local(): jnp.einsum('kic,kjc->ijc', panel_now, right_strip, preferred_element_type...]
  transfers between devices with their start and end apart: 10 -> 4, of which waited for: 10 -> 4; matrix products, arithmetic and copies ran while one was open for 4% -> 1% of each run, Pallas kernels for 0% -> 0%
where the time goes in v1:
time: 615 us; the launch traced here: 613 us
  waiting for transfers between devices  380 us (62%)
  Pallas kernels  85 us (14%)
  local copies, waits for them, and re-layouts  52.1 us (8%)
  matrix products  38.3 us (6%)
  blocking collectives  27.4 us (4%)
  between operations  13.8 us (2%)
  starting transfers between devices  8.59 us (1%)
  other arithmetic  8.13 us (1%)
    all_gather x2, waiting for transfers between devices, full_bias(): gathered = lax.all_gather(tile_bias, ('row', 'col'), axis=0, tiled=True)  363 us
    pallas_call x1, Pallas kernels, tri_call(): pl.pallas_call(tri_kernel, out_shape=jax.ShapeDtypeStruct((PX, CZ), F32),...  85 us
    dot_general x8, matrix products, one_head(): jnp.einsum('ijk,ikd->ijd', weight, values_head, preferred_element_type=jn...  17.4 us
    all_to_all x1, blocking collectives, local(): lax.all_to_all(update, 'row', split_axis=0, concat_axis=1, tiled=True)  14.5 us
    sub x8, matrix products, one_head(): scores = scores - jnp.max(scores, axis=-1, keepdims=True)  13.5 us
    all_to_all x1, blocking collectives, local(): lax.all_to_all(update, 'col', split_axis=1, concat_axis=0, tiled=True)  12.9 us
  transfers between devices with their start and end apart: 4, of which 4 were waited for; matrix products, arithmetic and copies ran while one was open for 1% of the time, Pallas kernels for 0%

profile of v1, /device:TPU:0, one launch (start us, length us, event | category | flops | bytes accessed | tf_op | source)
XLA Modules:
  0.0 613.2 jit_solution(2914787030273813536)
XLA Ops:
  6.5 0.7 convert_element_type.68
  7.4 0.8 dynamic_slice.40
  8.1 0.8 dynamic_slice.41
  9.4 1.1 copy-done
  10.5 0.9 copy-done.1
  11.4 0.8 copy-done.2
  12.3 0.8 copy-done.3
  13.1 0.7 copy-done.4
  13.8 85.0 %shard_map.100 = f32[1152,128]{1,0:T(8,128)S(1)} custom-call(f32[1152,128]{1,0:T(8,128)S(1)} %bitcast.258, f32[9,128]{1,0:T(8,128)S(1)} %mul.56.mask, s32[1152,128]{1,0:T(8,128)S(1)} %broadcast_in_dim.8.same, f32[2,128]{1,0:T(2,128)S(1)} %copy-done.4, bf16[2,128,512]{2,1,0:T(8,128)(2,1)S(1)} %copy-done.1, bf16[2,128,128]{2,1,0:T(8,128)(2,1)S(1)} %copy-done.2, ...), custom_call_target="tpu_custom_call" | custom-call | tf_op jit(solution)/shard_map/pallas_call | solution.py:169
  99.1 0.4 multiply_reduce_fusion.1
  99.9 3.0 convolution_bitcast_fusion.3
  102.9 0.7 copy.81
  103.8 1.1 divide_convert_fusion.5
  104.9 3.5 all-to-all-start
  108.7 0.7 slice_bitcast_fusion.6
  109.5 8.1 %all-to-all-done = bf16[48,24,128]{2,1,0:T(8,128)(2,1)S(1)} async-done(((bf16[48,24,128]{2,1,0:T(8,128)(2,1)}), bf16[48,24,128]{2,1,0:T(8,128)(2,1)S(1)}, u32[]{:S(2)}, u32[]{:S(2)}) %all-to-all-start) | async-done | bytes 294944 | tf_op jit(solution)/shard_map/all_to_all | solution.py:284
  117.7 0.5 fusion.107
  118.1 1.4 copy-done.6
  119.7 1.0 slice_bitcast_fusion.3
  120.6 181.9 %all-gather.3.cloned.1.call-done = f32[512,48,24]{1,2,0:T(8,128)} async-done(((f32[4,48,24]{1,2,0:T(8,128)}), f32[512,48,24]{1,2,0:T(8,128)}) %all-gather.3.cloned.1.call-update) | async-done | bytes 2359312 | tf_op jit(solution)/shard_map/all_gather | solution.py:206
  302.5 9.1 %copy.82 = f32[4,8,48,16,24]{2,1,4,3,0:T(8,128)} copy(f32[4,8,48,16,24]{2,4,0,3,1:T(8,128)} %bitcast.262) | data formatting | bytes 4718592 | tf_op jit(solution)/shard_map/transpose | solution.py:208
  311.6 4.8 reshape.176
  316.4 0.9 broadcast.109.clone2
  317.2 17.2 %while.20 = (s32[]{:T(128)}, f32[4,3,384,32]{2,3,0,1:T(8,128)}, bf16[4,3,384,32]{2,3,0,1:T(8,128)(2,1)}, bf16[4,3,384,32]{2,3,0,1:T(8,128)(2,1)}, f32[4,384,384]...) while((s32[]{:T(128)}, f32[4,3,384,32]{2,3,0,1:T(8,128)}, ...), condition=%wide.region_5.6_spmd, body=%wide.region_2.5_spmd.sunk | while | flops 89802624 | bytes 2890841 | solution.py:230
  317.3 1.7 fusion.136
  319.0 2.6 fusion.137
  321.6 1.7 fusion.136
  323.3 2.6 fusion.137
  325.9 1.7 fusion.136
  327.6 2.6 fusion.137
  330.2 1.7 fusion.136
  331.9 2.5 fusion.137
  334.4 1.4 fusion.86
  336.7 12.9 %all_to_all.48 = bf16[3,384,128]{2,0,1:T(4,128)(2,1)S(1)} all-to-all(bf16[3,384,128]{2,0,1:T(4,128)(2,1)S(1)} %copy.88), channel_id=1, replica_groups=mesh['row'=8,'col'=16] {'col'}, dimensions={1} | all-to-all | bytes 589824 | tf_op jit(solution)/shard_map/all_to_all | solution.py:288
  350.0 0.4 multiply_reduce_fusion
  350.9 3.0 convolution_bitcast_fusion.2
  353.8 0.7 copy.95
  355.2 0.8 copy.92
  355.9 4.8 all-to-all-start.2
  360.9 8.9 %all-to-all-done.2 = bf16[48,24,128]{2,0,1:T(8,128)(2,1)S(1)} async-done(((bf16[48,24,128]{2,0,1:T(8,128)(2,1)}), bf16[48,24,128]{2,0,1:T(8,128)(2,1)S(1)}, u32[]{:S(2)}, u32[]{:S(2)}) %all-to-all-start.2) | async-done | bytes 294944 | tf_op jit(solution)/shard_map/all_to_all | solution.py:292
  369.8 0.5 fusion.108
  370.3 1.4 copy-done.5
  371.9 0.8 slice_bitcast_fusion
  372.7 180.8 %all-gather.5.cloned.1.call-done = f32[512,48,24]{1,2,0:T(8,128)} async-done(((f32[4,48,24]{1,2,0:T(8,128)}), f32[512,48,24]{1,2,0:T(8,128)}) %all-gather.5.cloned.1.call-update) | async-done | bytes 2359312 | tf_op jit(solution)/shard_map/all_gather | solution.py:206
  553.5 9.1 %copy.127 = f32[8,16,4,48,24]{3,0,4,1,2:T(8,128)} copy(f32[8,16,4,48,24]{3,4,2,1,0:T(8,128)} %bitcast.263) | data formatting | bytes 4718592 | tf_op jit(solution)/shard_map/reshape | solution.py:207
  562.6 5.9 reshape.180
  568.5 19.3 %while.21 = (s32[]{:T(128)}, f32[4,3,384,32]{2,3,0,1:T(8,128)S(1)}, bf16[4,3,384,32]{2,3,0,1:T(8,128)(2,1)}, bf16[4,3,384,32]{2,3,0,1:T(8,128)(2,1)S(1)}, f32[4,...) while((s32[]{:T(128)}, f32[4,3,384,32]{2,3,0,1:T(8,128)S(1)}, ...), condition=%wide.region_11.12_spmd, body=%wide.region_8.11_spmd.sunk | while | flops 89802624 | bytes 4073049 | solution.py:230
  568.5 1.1 constant_dynamic-slice_fusion.2
  569.9 1.7 fusion.143
  571.5 1.8 fusion.144
  573.3 1.1 constant_dynamic-slice_fusion.2
  574.7 1.7 fusion.143
  576.3 1.8 fusion.144
  578.2 1.1 constant_dynamic-slice_fusion.2
  579.5 1.7 fusion.143
  581.2 1.8 fusion.144
  583.0 1.1 constant_dynamic-slice_fusion.2
  584.3 1.7 fusion.143
  586.0 1.8 fusion.144
  587.8 1.2 fusion.87
  589.0 0.8 copy.102
  589.8 0.6 reshape.181
  590.8 14.5 %all_to_all.49 = bf16[384,3,128]{2,1,0:T(4,128)(2,1)S(1)} all-to-all(bf16[384,3,128]{2,1,0:T(4,128)(2,1)S(1)} %reshape.182), channel_id=1, replica_groups=mesh['row'=8,'col'=16] {'row'}, dimensions={0} | all-to-all | bytes 589824 | tf_op jit(solution)/shard_map/all_to_all | solution.py:296
  605.3 1.0 copy_add_fusion
  (69 shorter events, 5.9 us)
Async XLA Ops:
  6.5 296.0 %all-gather.3.cloned.1.call-start = ((), (), s32[]{:S(2)}) async-start(), calls=%async_computation.4 | async-start | bytes 6340608 | tf_op jit(solution)/shard_map/all_gather | solution.py:206
  9.4 1.1 copy-start
  10.5 0.9 copy-start.1
  11.4 0.8 copy-start.2
  12.3 0.8 copy-start.3
  13.1 0.7 copy-start.4
  13.8 86.1 %copy-start.12 = (f32[2,128,4]{1,2,0:T(4,128)S(1)}, f32[2,128,4]{1,2,0:T(4,128)}, u32[]{:S(2)}) copy-start(f32[2,128,4]{1,2,0:T(4,128)} %param.22) | copy-start | bytes 12292
  99.5 9.2 %copy-start.8 = (bf16[2,128,512]{2,1,0:T(8,128)(2,1)S(1)}, bf16[2,128,512]{2,1,0:T(8,128)(2,1)}, u32[]{:S(2)}) copy-start(bf16[2,128,512]{2,1,0:T(8,128)(2,1)} %param.21) | copy-start | bytes 786436
  99.9 9.6 %copy-start.11 = (s32[384]{0:T(512)S(1)}, s32[384]{0:T(512)}, u32[]{:S(2)}) copy-start(s32[384]{0:T(512)} %param.16) | copy-start | bytes 4612
  104.9 12.7 %all-to-all-start = ((bf16[48,24,128]{2,1,0:T(8,128)(2,1)}), bf16[48,24,128]{2,1,0:T(8,128)(2,1)S(1)}, u32[]{:S(2)}, u32[]{:S(2)}) async-start(bf16[48,24,128]{2,1,0:T(8,128)(2,1)} %divide_convert_fusion.5), calls=%async_computation | async-start | bytes 589824 | tf_op jit(solution)/shard_map/all_to_all | solution.py:284
  108.5 445.0 %all-gather.5.cloned.1.call-start = ((), (), s32[]{:S(2)}) async-start(), calls=%async_computation.5 | async-start | bytes 6340608 | tf_op jit(solution)/shard_map/all_gather | solution.py:206
  118.1 1.4 copy-start.6
  334.4 1.8 copy-start.9
  350.8 9.9 %copy-start.7 = (bf16[512,128]{0,1:T(8,128)(2,1)S(1)}, bf16[512,128]{0,1:T(8,128)(2,1)}, u32[]{:S(2)}) copy-start(bf16[512,128]{0,1:T(8,128)(2,1)} %get-tuple-element.171) | copy-start | bytes 393220
  355.9 13.9 %all-to-all-start.2 = ((bf16[48,24,128]{2,0,1:T(8,128)(2,1)}), bf16[48,24,128]{2,0,1:T(8,128)(2,1)S(1)}, u32[]{:S(2)}, u32[]{:S(2)}) async-start(bf16[48,24,128]{2,0,1:T(8,128)(2,1)} %copy.92), calls=%async_computation.2 | async-start | bytes 589824 | tf_op jit(solution)/shard_map/all_to_all | solution.py:292
  370.3 1.4 copy-start.5
  589.0 1.4 copy-start.10
Sparse Core Ops, SparseCore 0:
  103.8 198.6 all-gather.2
  354.7 198.7 all-gather.4

commit v2 on v1

v2 whole, which is shorter than its diff:
```python
import jax
import jax.numpy as jnp
from jax import lax
from jax.sharding import PartitionSpec as P
from jax.experimental import pallas as pl
from jax.experimental.pallas import tpu as pltpu

F32 = jnp.float32
BF16 = jnp.bfloat16
MESH = pl.DeviceIdType.MESH
CZ = 128
ROWS, COLS = 8, 16
IL, JL = 48, 24
PX = IL * JL
NRES = 384
NDEV = ROWS * COLS
QS = PX // 128
HEADS, DH = 4, 32
STRIP = HEADS * 3 * JL
LINE0 = 80
LOG2E = 1.4426950408889634
SCALE = DH ** -0.5
GO, BACK = 32, 16
GO32, BACK32 = 24, 16


def normalize(v):
    mean = jnp.mean(v, axis=-1, keepdims=True)
    c = v - mean
    spread = jnp.mean(c * c, axis=-1, keepdims=True)
    return c * lax.rsqrt(spread + 1e-05)


def dot(a, b, dims=((1,), (0,))):
    return lax.dot_general(a, b, (dims, ((), ())), preferred_element_type=F32)


def exchange_start(src, dst, send, recv, r, s):
    me = r * COLS + s

    def go(d, _):
        p = jnp.bitwise_xor(me, d)
        pltpu.make_async_remote_copy(
            src_ref=src.at[p], dst_ref=dst.at[me], send_sem=send, recv_sem=recv,
            device_id=(p // COLS, p % COLS), device_id_type=MESH,
        ).start()
        return 0

    lax.fori_loop(1, NDEV, go, 0)
    dst[me] = src[me]


def exchange_wait(src, dst, send, recv):
    part = pl.ds(0, NDEV - 1)
    pltpu.make_async_copy(src.at[part], dst.at[part], recv).wait()
    pltpu.make_async_copy(src.at[part], dst.at[part], send).wait()


def triangle(t, x, mask, proj, gate, out, nb, stage, send_go, recv_go, send_back, recv_back, left, right, sems, r, s, before_send):
    def side(q, _):
        rows = pl.ds(pl.multiple_of(q * 128, 128), 128)
        n = normalize(x[rows, :]).astype(BF16)
        nb[rows, :] = n
        p = dot(n, proj[t])
        m = mask[pl.ds(q, 1), :]
        for k in range(2):
            v = jax.nn.sigmoid(p[:, (2 * k + 1) * CZ:(2 * k + 2) * CZ]) * p[:, 2 * k * CZ:(2 * k + 1) * CZ]
            stage[pl.ds(k * QS + q, CZ, stride=GO32), :] = v.T * m
        return 0

    lax.fori_loop(0, QS, side, 0)

    def pack(c, _):
        f = stage[pl.ds(pl.multiple_of(c * GO32, GO32), GO32), :]
        send_go[c] = jnp.concatenate([f, jnp.zeros((GO - GO32, 128), F32)], axis=0).astype(BF16)
        return 0

    lax.fori_loop(0, CZ, pack, 0, unroll=4)
    before_send()
    exchange_start(send_go, recv_go, sems.at[0], sems.at[1], r, s)
    exchange_wait(send_go, recv_go, sems.at[0], sems.at[1])

    def unpack(c, _):
        stage[pl.ds(pl.multiple_of(c * GO32, GO32), GO32), :] = recv_go[c].astype(F32)[:GO32]
        return 0

    lax.fori_loop(0, NDEV, unpack, 0, unroll=4)

    for k, ref in enumerate((left, right)):
        def gather(a, _):
            v = []
            for rr in range(ROWS):
                v.append(jnp.concatenate(
                    [stage[pl.ds(rr * COLS * GO32 + k * QS + 3 * a + i, COLS, stride=GO32), :] for i in range(3)], axis=1))
            for b in range(8):
                row = jnp.concatenate([u[:, IL * b:IL * (b + 1)] for u in v], axis=1)
                for i in range(3):
                    ref[pl.ds(i * NRES + 8 * a + b, COLS, stride=JL), :] = row[:, 128 * i:128 * (i + 1)]
            return 0

        lax.fori_loop(0, 3, gather, 0)
    lf = jnp.concatenate([left[pl.ds(i * NRES, NRES), :] for i in range(3)], axis=1).astype(BF16)
    rt = jnp.concatenate([right[pl.ds(i * NRES, NRES), :] for i in range(3)], axis=1).astype(BF16)
    prod = dot(rt, lf, ((0,), (0,))) if t == 0 else dot(rt, lf, ((1,), (1,)))
    for i in range(3):
        left[pl.ds(i * NRES, NRES), :] = prod[:, 128 * i:128 * (i + 1)]

    def scatter(a, _):
        v = []
        for b in range(8):
            v.append(jnp.concatenate([left[pl.ds(i * NRES + 8 * a + b, COLS, stride=JL), :] for i in range(3)], axis=1))
        for rr in range(ROWS):
            row = jnp.concatenate([u[:, IL * rr:IL * (rr + 1)] for u in v], axis=1)
            for i in range(3):
                stage[pl.ds(rr * COLS * BACK32 + 3 * a + i, COLS, stride=BACK32), :] = row[:, 128 * i:128 * (i + 1)]
        return 0

    lax.fori_loop(0, 3, scatter, 0)

    def pack2(c, _):
        send_back[c] = stage[pl.ds(pl.multiple_of(c * BACK32, BACK32), BACK32), :].astype(BF16)
        return 0

    lax.fori_loop(0, NDEV, pack2, 0, unroll=4)
    exchange_start(send_back, recv_back, sems.at[2], sems.at[3], r, s)
    exchange_wait(send_back, recv_back, sems.at[2], sems.at[3])

    def unpack2(c, _):
        stage[pl.ds(pl.multiple_of(c * BACK32, BACK32), BACK32), :] = recv_back[c].astype(F32)
        return 0

    lax.fori_loop(0, CZ, unpack2, 0, unroll=4)

    def finish(q, _):
        rows = pl.ds(pl.multiple_of(q * 128, 128), 128)
        pr = stage[pl.ds(q, CZ, stride=BACK32), :].T
        mixed = normalize(pr).astype(BF16)
        g = jax.nn.sigmoid(dot(nb[rows, :], gate[t]))
        x[rows, :] = x[rows, :] + g * dot(mixed, out[t])
        return 0

    lax.fori_loop(0, QS, finish, 0)

def group_start(axis, src, dst, send, recv, r, s):
    n, me = (ROWS, r) if axis == "row" else (COLS, s)

    def go(d, _):
        p = jnp.bitwise_xor(me, d)
        pltpu.make_async_remote_copy(
            src_ref=src(p), dst_ref=dst(me), send_sem=send, recv_sem=recv,
            device_id=(p, s) if axis == "row" else (r, p), device_id_type=MESH,
        ).start()
        return 0

    lax.fori_loop(1, n, go, 0)


def drain(ref, count, sem):
    part = ref.at[pl.ds(0, count)]
    pltpu.make_async_copy(part, part, sem).wait()


def strip(ref, slot):
    return ref.at[pl.ds(pl.multiple_of(slot * STRIP, 8), STRIP)]


def attention(t, x, kb, bias_w, w_project, w_out, nf, p1, bias, msg, got, upd, back, line, qs, ks, vs, gs, vt, us, sems, slots, r, s):
    axis, peers, per = ("col", COLS, LINE0) if t == 0 else ("row", ROWS, 3 * IL)
    xl, rest = s // 8, s % 8
    yy, core = rest // 2, rest % 2

    def at(dx, dy, dc):
        return ((xl + dx) % 2) * 8 + ((yy + dy) % 4) * 2 + (core + dc) % 2

    def chunk(q, _):
        rows = pl.ds(pl.multiple_of(q * 128, 128), 128)
        n = normalize(x[rows, :])
        nf[rows, :] = n
        b8 = lax.dot_general(bias_w[t], n, (((1,), (1,)), ((), ())), precision=lax.Precision.HIGHEST, preferred_element_type=F32)
        p1[r, q] = (b8[:HEADS] + kb[t, pl.ds(q, 1), :]) * LOG2E
        return 0

    lax.fori_loop(0, QS, chunk, 0)
    group_start("row", lambda p: p1.at[r], lambda m: p1.at[m], sems.at[0], sems.at[1], r, s)

    if t == 0:
        for p in range(COLS):
            v = [nf[pl.ds(3 * p + u, JL, stride=IL), :] for u in range(3)]
            msg[p] = jnp.concatenate(v + [jnp.zeros((LINE0 - 72, CZ), F32)], axis=0).astype(BF16)
    else:
        for p in range(ROWS):
            msg[p] = nf[pl.ds(p * per, per), :].astype(BF16)
    group_start(axis, lambda p: msg.at[p], lambda m: got.at[m], sems.at[2], sems.at[3], r, s)
    me = s if t == 0 else r
    got[me] = msg[me]

    drain(p1, ROWS - 1, sems.at[1])

    def lay(a, _):
        v = [jnp.concatenate([p1[rr, 3 * a + i] for i in range(3)], axis=1) for rr in range(ROWS)]
        for b in range(8):
            row = jnp.concatenate([u[:, IL * b:IL * (b + 1)] for u in v], axis=1)
            for i in range(3):
                bias[pl.ds(s * STRIP + i * JL + 8 * a + b, HEADS, stride=3 * JL), :] = row[:, 128 * i:128 * (i + 1)]
        return 0

    lax.fori_loop(0, 3, lay, 0)

    def pass_on(slot, target):
        pltpu.make_async_remote_copy(
            src_ref=strip(bias, slot), dst_ref=strip(bias, slot), send_sem=sems.at[4], recv_sem=slots.at[slot],
            device_id=(r, target), device_id_type=MESH,
        ).start()

    def arrived(slot):
        pltpu.make_async_copy(strip(bias, slot), strip(bias, slot), slots.at[slot]).wait()

    for d in ((1, 0, 0), (0, 1, 0), (0, 3, 0), (0, 2, 0), (0, 0, 1)):
        pass_on(s, at(*d))

    drain(got, peers - 1, sems.at[3])
    if t == 0:
        for p in range(COLS):
            v = got[p].astype(F32)
            for u in range(3):
                line[pl.ds(u * NRES + p * JL, JL), :] = v[u * JL:(u + 1) * JL]
    else:
        for p in range(ROWS):
            for u in range(3):
                line[pl.ds(u * NRES + p * IL, IL), :] = got[p, u * IL:(u + 1) * IL, :].astype(F32)

    def project(u):
        rows = pl.ds(u * NRES, NRES)
        p = dot(line[rows, :].astype(BF16), w_project[t])
        qs[rows, :] = p[:, :CZ].astype(BF16)
        ks[rows, :] = p[:, CZ:2 * CZ].astype(BF16)
        v = p[:, 2 * CZ:3 * CZ]
        if t == 0:
            vt[pl.ds(u * CZ, CZ), :] = v.T.astype(BF16)
        else:
            vs[rows, :] = v.astype(BF16)
        gs[rows, :] = jax.nn.sigmoid(p[:, 3 * CZ:])

    project(0)
    arrived(at(1, 0, 0))
    for d in ((0, 1, 0), (0, 3, 0), (0, 0, 1)):
        pass_on(at(1, 0, 0), at(*d))
    arrived(at(0, 2, 0))
    for d in ((1, 0, 0), (0, 0, 1)):
        pass_on(at(0, 2, 0), at(*d))
    project(1)
    for d in ((0, 1, 0), (0, 3, 0), (1, 1, 0), (1, 3, 0), (1, 2, 0)):
        arrived(at(*d))
        pass_on(at(*d), at(0, 0, 1))
    project(2)
    for dx in range(2):
        for dy in range(4):
            arrived(at(dx, dy, 1))

    lane_head = lax.broadcasted_iota(jnp.int32, (1, CZ), 1) // DH

    def scores_max(e):
        return jnp.exp2(e - jnp.max(e, axis=0 if t == 0 else 1, keepdims=True))

    if t == 0:
        def tile(n, _):
            u, i = n // 3, n % 3
            qrow = pl.ds(pl.multiple_of(n * 128, 128), 128)
            q = qs[qrow, :]
            k = ks[pl.ds(pl.multiple_of(u * NRES, 128), NRES), :]
            parts = []
            for h in range(HEADS):
                qh = jnp.where(lane_head == h, q, jnp.zeros_like(q))
                b = jnp.concatenate([bias[pl.ds(pl.multiple_of(p * STRIP + h * 3 * JL + i * JL, 8), JL), :] for p in range(COLS)], axis=0)
                e = scores_max(dot(k, qh, ((1,), (1,))) * (SCALE * LOG2E) + b)
                total = jnp.sum(e, axis=0, keepdims=True)
                o = dot(vt[pl.ds(pl.multiple_of(u * CZ + h * DH, DH), DH), :], e.astype(BF16))
                parts.append(o / total)
            att = jnp.concatenate(parts, axis=0).T
            gated = (gs[qrow, :] * att).astype(BF16)
            us[qrow, :] = dot(gated, w_out[t])
            return 0

        lax.fori_loop(0, 9, tile, 0)
        for p in range(COLS):
            v = [us[pl.ds(u * NRES + p * JL, JL), :] for u in range(3)]
            upd[p] = jnp.concatenate(v + [jnp.zeros((LINE0 - 72, CZ), F32)], axis=0).astype(BF16)
    else:
        def tile(n, _):
            u, i = n // 4, n % 4
            qrow = pl.ds(pl.multiple_of(n * 96, 32), 96)
            lrow = pl.ds(pl.multiple_of(u * NRES, 128), NRES)
            q, k, v = qs[qrow, :], ks[lrow, :], vs[lrow, :]
            att = jnp.zeros((96, CZ), F32)
            for h in range(HEADS):
                kh = jnp.where(lane_head == h, k, jnp.zeros_like(k))
                vh = jnp.concatenate([jnp.where(lane_head == h, v, jnp.zeros_like(v)), jnp.ones_like(v)], axis=1)
                b = jnp.concatenate([
                    jnp.concatenate([bias[pl.ds(pl.multiple_of((4 * i + p) * STRIP + h * 3 * JL + w * JL, 8), JL), :] for p in range(4)], axis=0)
                    for w in range(3)], axis=1)
                e = scores_max(dot(q, kh, ((1,), (1,))) * (SCALE * LOG2E) + b)
                o = dot(e.astype(BF16), vh)
                att = att + o[:, :CZ] / o[:, CZ:]
            gated = (gs[qrow, :] * att).astype(BF16)
            us[qrow, :] = dot(gated, w_out[t])
            return 0

        lax.fori_loop(0, 12, tile, 0)
        for p in range(ROWS):
            for u in range(3):
                upd[p, u * IL:(u + 1) * IL, :] = us[pl.ds(u * NRES + p * IL, IL), :].astype(BF16)

    group_start(axis, lambda p: upd.at[p], lambda m: back.at[m], sems.at[5], sems.at[6], r, s)
    back[me] = upd[me]
    drain(back, peers - 1, sems.at[6])
    if t == 0:
        for p in range(COLS):
            v = back[p].astype(F32)
            for u in range(3):
                rows = pl.ds(3 * p + u, JL, stride=IL)
                x[rows, :] = x[rows, :] + v[u * JL:(u + 1) * JL]
    else:
        for p in range(ROWS):
            rows = pl.ds(p * per, per)
            x[rows, :] = x[rows, :] + back[p].astype(F32)
    drain(p1, ROWS - 1, sems.at[0])
    drain(msg, peers - 1, sems.at[2])
    pltpu.make_async_copy(bias.at[pl.ds(0, 15 * STRIP)], bias.at[pl.ds(0, 15 * STRIP)], sems.at[4]).wait()
    drain(upd, peers - 1, sems.at[5])


def kernel(pair, mask, kb, same, table, proj, gate, out, att_w, bias_w, att_o, y, x, nb, stage,
           sg0, rg0, sb0, rb0, sg1, rg1, sb1, rb1, left, right, *more):
    att0, att1, shared, sems, asems, slots = more[:6], more[6:12], more[12:20], more[20], more[21], more[22]
    r = lax.axis_index("row")
    s = lax.axis_index("col")
    me = r * COLS + s
    barrier = pltpu.get_barrier_semaphore()

    def greet(d, _):
        p = jnp.bitwise_xor(me, d)
        pl.semaphore_signal(barrier, inc=1, device_id=(p // COLS, p % COLS), device_id_type=MESH)
        return 0

    lax.fori_loop(1, NDEV, greet, 0)
    stage[...] = jnp.zeros_like(stage)
    for j in range(JL):
        part = pl.ds(j * IL, IL)
        x[part, :] = pair[pl.ds(j, IL, stride=JL), :] + jnp.where(same[part, :] > 0, table[1:2, :], table[0:1, :])
    triangle(0, x, mask, proj, gate, out, nb, stage, sg0, rg0, sb0, rb0, left, right, sems.at[0], r, s,
             lambda: pl.semaphore_wait(barrier, NDEV - 1))
    triangle(1, x, mask, proj, gate, out, nb, stage, sg1, rg1, sb1, rb1, left, right, sems.at[1], r, s, lambda: None)
    for t, bufs in ((0, att0), (1, att1)):
        nf, line, qs, ks, vs, gs, vt, us = shared
        attention(t, x, kb, bias_w, att_w, att_o, nf, *bufs, line, qs, ks, vs, gs, vt, us, asems.at[t], slots.at[t], r, s)
    for j in range(JL):
        y[pl.ds(j, IL, stride=JL), :] = x[pl.ds(j * IL, IL), :]


def call(*args):
    vm = pl.BlockSpec(memory_space=pltpu.VMEM)
    bufs = []
    for _ in range(2):
        bufs += [pltpu.VMEM((NDEV, GO, 128), BF16)] * 2 + [pltpu.VMEM((NDEV, BACK, 128), BF16)] * 2
    lines = [
        [pltpu.VMEM((ROWS, QS, HEADS, 128), F32), pltpu.VMEM((COLS * STRIP, 128), F32)]
        + [pltpu.VMEM(shape, BF16)] * 4
        for shape in ((COLS, LINE0, CZ), (ROWS, 3 * IL, CZ))
    ]
    tall = (3 * NRES, 128)
    return pl.pallas_call(
        kernel,
        out_shape=jax.ShapeDtypeStruct((PX, CZ), F32),
        in_specs=[vm] * len(args),
        out_specs=vm,
        scratch_shapes=[
            pltpu.VMEM((PX, CZ), F32),
            pltpu.VMEM((PX, CZ), BF16),
            pltpu.VMEM((NDEV * GO32, 128), F32),
            *bufs,
            pltpu.VMEM(tall, F32),
            pltpu.VMEM(tall, F32),
            *lines[0],
            *lines[1],
            pltpu.VMEM((PX, CZ), F32),
            pltpu.VMEM(tall, F32),
            pltpu.VMEM(tall, BF16),
            pltpu.VMEM(tall, BF16),
            pltpu.VMEM(tall, BF16),
            pltpu.VMEM(tall, F32),
            pltpu.VMEM((3 * CZ, NRES), BF16),
            pltpu.VMEM(tall, F32),
            pltpu.SemaphoreType.DMA((2, 4)),
            pltpu.SemaphoreType.DMA((2, 7)),
            pltpu.SemaphoreType.DMA((2, COLS)),
        ],
        compiler_params=pltpu.CompilerParams(collective_id=0, has_side_effects=True, vmem_limit_bytes=56 << 20),
    )(*args)


def local(pair_rep, chain_id, live_mask, chain_table, tri_proj, tri_gate, tri_out, att_project, att_bias, att_out):
    row_index = lax.axis_index("row")
    col_index = lax.axis_index("col")
    chain_rows = lax.dynamic_slice_in_dim(chain_id, row_index * IL, IL)
    chain_cols = lax.dynamic_slice_in_dim(chain_id, col_index * JL, JL)
    live = live_mask.astype(F32)
    live_rows = lax.dynamic_slice_in_dim(live, row_index * IL, IL)
    live_cols = lax.dynamic_slice_in_dim(live, col_index * JL, JL)
    mask = (live_cols[:, None] * live_rows[None, :]).reshape(QS, 128)
    zero = jnp.zeros((JL, IL), F32)
    key_bias = jnp.stack([zero + ((live_cols - 1.0) * 1e9)[:, None], zero + ((live_rows - 1.0) * 1e9)[None, :]]).reshape(2, QS, 128)
    same = (chain_cols[:, None] == chain_rows[None, :]).reshape(PX, 1)
    same = jnp.broadcast_to(same, (PX, CZ)).astype(jnp.int32)
    bias_w = jnp.pad(jnp.swapaxes(att_bias, 1, 2), ((0, 0), (0, 8 - HEADS), (0, 0)))
    pair_out = call(
        pair_rep.reshape(PX, CZ), mask, key_bias, same, chain_table, tri_proj, tri_gate, tri_out,
        att_project, bias_w, att_out,
    )
    return pair_out.reshape(pair_rep.shape)


def solution(mesh):
    return jax.shard_map(
        local,
        mesh=mesh,
        in_specs=(P("row", "col", None), P(), P(), P(), P(), P(), P(), P(), P(), P()),
        out_specs=P("row", "col", None),
        check_vma=False,
    )
```

time: 615 us -> 180 us (0.29)
  waiting for transfers between devices: 380 us -> 0 us
  Pallas kernels: 85 us -> 171 us
  local copies, waits for them, and re-layouts: 52.1 us -> 7.11 us
  matrix products: 38.3 us -> 0 us
  blocking collectives: 27.4 us -> 0 us
  between operations: 13.8 us -> 0.02 us
  starting transfers between devices: 8.59 us -> 0 us
  other arithmetic: 8.13 us -> 0.31 us
    all_gather x2 -> x0, waiting for transfers between devices: 363 us -> none  [full_bias(): gathered = lax.all_gather(tile_bias, ('row', 'col'), axis=0, tiled=True)]
    pallas_call x1, Pallas kernels: 85 us -> 171 us  [call(): pl.pallas_call(kernel, out_shape=jax.ShapeDtypeStruct((PX, CZ), F32), in_...]
    all_to_all x2 -> x0, blocking collectives: 27.4 us -> none  [the longest x1 14.5 us: local(): lax.all_to_all(update, 'row', split_axis=0, concat_axis=1, tiled=True)]
    dot_general x14 -> x0, matrix products: 24.8 us -> none  [the longest x8 17.4 us: one_head(): jnp.einsum('ijk,ikd->ijd', weight, values_head, preferred_element_type=jn...]
    reshape x6 -> x1, local copies, waits for them, and re-layouts: 20.7 us -> 0.68 us  [local(): jnp.stack([zero + ((live_cols - 1.0) * 1000000000.0)[:, None], zero + ((l...]
    all_to_all x2 -> x0, waiting for transfers between devices: 17 us -> none  [the longest x1 8.93 us: local(): lax.all_to_all(normed.astype(jnp.bfloat16), 'row', split_axis=1, concat_a...]
    sub x8 -> x0, matrix products: 13.5 us -> none  [one_head(): scores = scores - jnp.max(scores, axis=-1, keepdims=True)]
    transpose x5 -> x0, local copies, waits for them, and re-layouts: 10.8 us -> none  [the longest x1 9.08 us: full_bias(): gathered = jnp.transpose(gathered, (2, 0, 3, 1, 4))]
  transfers between devices with their start and end apart: 4 -> 0, of which waited for: 4 -> 0; matrix products, arithmetic and copies ran while one was open for 1% -> 0% of each run, Pallas kernels for 0% -> 0%
where the time goes in v2:
time: 180 us; the launch traced here: 179 us
  Pallas kernels  171 us (95%)
  local copies, waits for them, and re-layouts  7.11 us (4%)
    pallas_call x1, Pallas kernels, call(): pl.pallas_call(kernel, out_shape=jax.ShapeDtypeStruct((PX, CZ), F32), in_...  171 us
    unnamed x7, local copies, waits for them, and re-layouts  3.82 us

profile of v2, /device:TPU:0, one launch (start us, length us, event | category | flops | bytes accessed | tf_op | source)
XLA Modules:
  0.0 178.9 jit_solution(8407392193761357349)
XLA Ops:
  0.0 0.0 copy-start.2
  0.0 0.7 copy-done.2
  0.7 0.0 copy-start.1
  0.7 0.1 dynamic_slice.15
  0.8 0.1 dynamic_slice.14
  0.8 0.5 copy-done.1
  1.4 0.1 add_multiply_fusion
  1.4 0.1 add_multiply_fusion.1
  1.5 0.0 copy-start
  1.5 0.7 copy-done
  2.2 0.6 pad.4.bias_w
  2.8 0.1 compare_convert_fusion
  2.9 0.1 reshape.39
  3.0 0.1 broadcast_multiply_fusion
  3.0 0.7 mul.39.mask
  3.7 0.1 stack.9
  3.8 0.7 reshape.37.kb
  4.5 1.0 broadcast_in_dim.2.same
  5.5 171.5 %shard_map.100 = f32[1152,128]{1,0:T(8,128)} custom-call(f32[1152,128]{1,0:T(8,128)} %bitcast.4, f32[9,128]{1,0:T(8,128)} %mul.39.mask, f32[2,9,128]{2,1,0:T(8,128)} %reshape.37.kb, s32[1152,128]{1,0:T(8,128)} %broadcast_in_dim.2.same, f32[2,128]{1,0:T(2,128)} %table.1, bf16[2,128,512]{2,1,0:T(8,128)(2,1)} %proj.1, bf16[2,128,128]{2,1,0:T(8,128)(2,1)} %gate.1, ...), custom_call_target="tpu_custom_call" | custom-call | tf_op jit(solution)/shard_map/pallas_call | solution.py:371
  177.0 1.9 %copy.12 = f32[48,24,128]{2,1,0:T(8,128)} copy(f32[48,24,128]{2,1,0:T(8,128)} %bitcast.3) | data formatting | bytes 1179648
  (3 shorter events, 0.0 us)
Async XLA Ops:
  0.0 0.7 copy-start.2
  0.7 0.7 copy-start.1
  1.5 0.7 copy-start

commit v3 on v0

v3 whole, which is shorter than its diff:
```python
import jax
import jax.numpy as jnp
from jax import lax
from jax.sharding import PartitionSpec as P
from jax.experimental import pallas as pl
from jax.experimental.pallas import tpu as pltpu

F32 = jnp.float32
BF16 = jnp.bfloat16
MESH = pl.DeviceIdType.MESH
CZ = 128
ROWS, COLS = 8, 16
IL, JL = 48, 24
PX = IL * JL
NRES = 384
QS = PX // 128
PARTS = 3
HEADS, DH = 4, 32
STRIP = 3 * JL
LINE0 = 80
LOG2E = 1.4426950408889634
SCALE = DH ** -0.5


def normalize(v):
    mean = jnp.mean(v, axis=-1, keepdims=True)
    c = v - mean
    spread = jnp.mean(c * c, axis=-1, keepdims=True)
    return c * lax.rsqrt(spread + 1e-05)


def dot(a, b, dims=((1,), (0,))):
    return lax.dot_general(a, b, (dims, ((), ())), preferred_element_type=F32)


def repeat(n, body, first=0):
    def step(i, carry):
        body(i)
        return carry

    lax.fori_loop(first, n, step, 0)


def to_peers(axis, r, s, act):
    n, me = (ROWS, r) if axis == "row" else (COLS, s)

    def one(d):
        p = jnp.bitwise_xor(me, d)
        act(p, (p, s) if axis == "row" else (r, p))

    repeat(n, one, 1)


def scatter_to(axis, src, dst, send, recv, r, s):
    to_peers(axis, r, s, lambda p, device: pltpu.make_async_remote_copy(
        src_ref=src(p), dst_ref=dst, send_sem=send, recv_sem=recv, device_id=device, device_id_type=MESH
    ).start())


def drain(ref, sem):
    pltpu.make_async_copy(ref, ref, sem).wait()


def three(a):
    return pl.ds(3 * a, 3)


class Triangle:
    SHAPES = [
        ((ROWS, QS, 32, 128), BF16), ((ROWS, QS, 32, 128), BF16),
        ((COLS, QS, 16, 128), BF16), ((COLS, QS, 16, 128), BF16),
        ((COLS, PARTS, 32, 128), BF16), ((COLS, PARTS, 32, 128), BF16),
        ((ROWS, QS, 16, 128), BF16), ((ROWS, QS, 16, 128), BF16),
    ]

    def __init__(self, t, x, nb, mask, weights, bufs, stage, left, right, sends, recvs, r, s):
        self.t, self.x, self.nb, self.mask, self.r, self.s = t, x, nb, mask, r, s
        self.proj, self.gate, self.out = weights
        self.s1, self.r1, self.s2, self.r2, self.s3, self.r3, self.s4, self.r4 = bufs
        self.stage, self.left, self.right, self.sends, self.recvs = stage, left, right, sends, recvs

    def side(self, a):
        r, s = self.r, self.s

        def chunk(i, _):
            q = 3 * a + i
            rows = pl.ds(pl.multiple_of(q * 128, 128), 128)
            n = normalize(self.x[rows, :]).astype(BF16)
            self.nb[rows, :] = n
            p = dot(n, self.proj[self.t])
            m = self.mask[pl.ds(q, 1), :]
            for k in range(2):
                v = jax.nn.sigmoid(p[:, (2 * k + 1) * CZ:(2 * k + 2) * CZ]) * p[:, 2 * k * CZ:(2 * k + 1) * CZ]
                v = (v.T * m).astype(BF16)
                for p_ in range(ROWS):
                    self.s1[p_, q, 16 * k:16 * k + 16, :] = v[16 * p_:16 * p_ + 16]
            return 0

        lax.fori_loop(0, 3, chunk, 0)
        scatter_to("row", lambda p: self.s1.at[p, three(a)], self.r1.at[r, three(a)], self.sends.at[0], self.recvs.at[0, a], r, s)
        self.r1[r, three(a)] = self.s1[r, three(a)]

    def relay(self, a):
        r, s, mid = self.r, self.s, self.stage
        drain(self.r1.at[pl.ds(0, ROWS - 1), three(a)], self.recvs.at[0, a])

        def chunk(i, _):
            q = 3 * a + i
            for p in range(ROWS):
                v = self.r1[p, q].astype(F32)
                for k in range(2):
                    mid[pl.ds(i * 256 + k * 8 + p, 16, stride=16), :] = v[16 * k:16 * k + 16]
            for c in range(16):
                self.s2[c, q] = mid[pl.ds(pl.multiple_of(i * 256 + c * 16, 16), 16), :].astype(BF16)
            return 0

        lax.fori_loop(0, 3, chunk, 0)
        scatter_to("col", lambda p: self.s2.at[p, three(a)], self.r2.at[s, three(a)], self.sends.at[1], self.recvs.at[1, a], r, s)
        self.r2[s, three(a)] = self.s2[s, three(a)]

    def gather(self, a):
        f = self.stage
        drain(self.r2.at[pl.ds(0, COLS - 1), three(a)], self.recvs.at[1, a])
        for i in range(3):
            for p in range(COLS):
                f[i * 256 + p * 16:i * 256 + p * 16 + 16, :] = self.r2[p, 3 * a + i].astype(F32)
        for k, ref in enumerate((self.left, self.right)):
            v = [jnp.concatenate([f[pl.ds(i * 256 + k * 8 + p, COLS, stride=16), :] for i in range(3)], axis=1) for p in range(ROWS)]
            for b in range(8):
                row = jnp.concatenate([u[:, IL * b:IL * (b + 1)] for u in v], axis=1)
                for i in range(3):
                    ref[pl.ds(i * NRES + 8 * a + b, COLS, stride=JL), :] = row[:, 128 * i:128 * (i + 1)]

    def multiply(self):
        lf, rt = (jnp.concatenate([ref[pl.ds(i * NRES, NRES), :] for i in range(3)], axis=1).astype(BF16) for ref in (self.left, self.right))
        prod = dot(rt, lf, ((0,), (0,))) if self.t == 0 else dot(rt, lf, ((1,), (1,)))
        for i in range(3):
            self.left[pl.ds(i * NRES, NRES), :] = prod[:, 128 * i:128 * (i + 1)]

    def give(self, a):
        r, s = self.r, self.s
        for p in range(COLS):
            v = [self.left[pl.ds(i * NRES + JL * p + 8 * a, 8), :] for i in range(3)]
            self.s3[p, a] = jnp.concatenate(v + [jnp.zeros((8, 128), F32)], axis=0).astype(BF16)
        scatter_to("col", lambda p: self.s3.at[p, a], self.r3.at[s, a], self.sends.at[2], self.recvs.at[2, a], r, s)
        self.r3[s, a] = self.s3[s, a]

    def relay_back(self, a):
        r, s, f = self.r, self.s, self.stage
        drain(self.r3.at[pl.ds(0, COLS - 1), a], self.recvs.at[2, a])
        for c in range(COLS):
            f[c * 32:c * 32 + 32, :] = self.r3[c, a].astype(F32)
        v = [jnp.concatenate([f[pl.ds(i * 8 + b, 16, stride=32), :] for i in range(3)], axis=1) for b in range(8)]
        for p in range(ROWS):
            row = jnp.concatenate([u[:, IL * p:IL * (p + 1)] for u in v], axis=1).astype(BF16)
            for i in range(3):
                self.s4[p, 3 * a + i] = row[:, 128 * i:128 * (i + 1)]
        scatter_to("row", lambda p: self.s4.at[p, three(a)], self.r4.at[r, three(a)], self.sends.at[3], self.recvs.at[3, a], r, s)
        self.r4[r, three(a)] = self.s4[r, three(a)]

    def finish(self, a):
        drain(self.r4.at[pl.ds(0, ROWS - 1), three(a)], self.recvs.at[3, a])

        def chunk(i, _):
            q = 3 * a + i
            rows = pl.ds(pl.multiple_of(q * 128, 128), 128)
            pr = jnp.concatenate([self.r4[p, q] for p in range(ROWS)], axis=0).astype(F32).T
            mixed = normalize(pr).astype(BF16)
            g = jax.nn.sigmoid(dot(self.nb[rows, :], self.gate[self.t]))
            self.x[rows, :] = self.x[rows, :] + g * dot(mixed, self.out[self.t])
            return 0

        lax.fori_loop(0, 3, chunk, 0)

    def middle(self):
        for step in (self.relay, self.gather):
            repeat(PARTS, step)
        self.multiply()
        for step in (self.give, self.relay_back):
            repeat(PARTS, step)

    def close(self):
        drain(self.s1.at[pl.ds(0, ROWS - 1)], self.sends.at[0])
        drain(self.s2.at[pl.ds(0, COLS - 1)], self.sends.at[1])
        drain(self.s3.at[pl.ds(0, COLS - 1)], self.sends.at[2])
        drain(self.s4.at[pl.ds(0, ROWS - 1)], self.sends.at[3])


class Attention:
    @staticmethod
    def shapes(t):
        msg = (COLS, LINE0, CZ) if t == 0 else (ROWS, 3 * IL, CZ)
        return [((ROWS, QS, HEADS, 128), F32), ((COLS * HEADS * STRIP, 128), F32)] + [(msg, BF16)] * 4

    SHARED = [
        ((PX, CZ), F32), ((PX, CZ), F32), ((PX, CZ), BF16), ((PX, CZ), BF16), ((PX, CZ), BF16), ((PX, CZ), F32),
        ((3 * CZ, NRES), BF16), ((PX, CZ), F32), ((3 * CZ, NRES), F32), ((PX, CZ), F32),
    ]

    def __init__(self, t, x, kb, weights, bufs, shared, sems, slots, r, s):
        self.t, self.x, self.kb, self.sems, self.slots, self.r, self.s = t, x, kb, sems, slots, r, s
        self.bias_w, self.w_project, self.w_out = weights
        self.p1, self.bias, self.msg, self.got, self.upd, self.back = bufs
        self.nf, self.line, self.qs, self.ks, self.vs, self.gs, self.vt, self.us, self.ot, self.acc = shared

    def chunk(self, a):
        t, r, s = self.t, self.r, self.s

        def one(i, _):
            q = 3 * a + i
            rows = pl.ds(pl.multiple_of(q * 128, 128), 128)
            n = normalize(self.x[rows, :])
            self.nf[rows, :] = n
            b8 = lax.dot_general(self.bias_w[t], n, (((1,), (1,)), ((), ())), precision=lax.Precision.HIGHEST, preferred_element_type=F32)
            self.p1[r, q] = (b8[:HEADS] + self.kb[t, pl.ds(q, 1), :]) * LOG2E
            return 0

        lax.fori_loop(0, 3, one, 0)
        mine = self.p1.at[r, three(a)]
        scatter_to("row", lambda p: mine, mine, self.sems.at[0], self.sems.at[4 + a], r, s)

    def at(self, dx, dy, dc):
        x, y, c = self.s // 8, (self.s % 8) // 2, self.s % 2
        return ((x + dx) % 2) * 8 + ((y + dy) % 4) * 2 + (c + dc) % 2

    def piece(self, slot, h):
        return self.bias.at[pl.ds(pl.multiple_of((slot * HEADS + h) * STRIP, 8), STRIP)]

    def arrived(self, d, h):
        drain(self.piece(self.at(*d), h), self.slots.at[self.at(*d), h])

    def pass_on(self, d, h, *targets):
        slot = self.at(*d)
        for target in targets:
            pltpu.make_async_remote_copy(
                src_ref=self.piece(slot, h), dst_ref=self.piece(slot, h), send_sem=self.sems.at[2], recv_sem=self.slots.at[slot, h],
                device_id=(self.r, self.at(*target)), device_id_type=MESH,
            ).start()

    def forward(self, h, step):
        across, up, down, other = (1, 0, 0), (0, 1, 0), (0, 3, 0), (0, 0, 1)
        if step == 0:
            self.arrived(across, h)
            self.pass_on(across, h, up, down, other)
            self.arrived(up, h)
            self.pass_on(up, h, other)
            self.arrived(down, h)
            self.pass_on(down, h, other)
            pl.when(h < 2)(lambda: self.pass_on(up, h, down))
            pl.when(h >= 2)(lambda: self.pass_on(down, h, up))
        elif step == 1:
            self.arrived((0, 2, 0), h)
            self.pass_on((0, 2, 0), h, across, other)
            for d in ((1, 1, 0), (1, 3, 0)):
                self.arrived(d, h)
                self.pass_on(d, h, other)
        elif step == 2:
            self.arrived((1, 2, 0), h)
            self.pass_on((1, 2, 0), h, other)
        else:
            repeat(8, lambda n: self.arrived((n // 4, n % 4, 1), h))

    def lines_out(self):
        if self.t == 0:
            for p in range(COLS):
                v = [self.nf[pl.ds(3 * p + u, JL, stride=IL), :] for u in range(3)]
                self.msg[p] = jnp.concatenate(v + [jnp.zeros((LINE0 - 72, CZ), F32)], axis=0).astype(BF16)
        else:
            for p in range(ROWS):
                self.msg[p] = self.nf[pl.ds(p * 3 * IL, 3 * IL), :].astype(BF16)
        scatter_to(self.axis(), lambda p: self.msg.at[p], self.got.at[self.me()], self.sems.at[1], self.sems.at[7], self.r, self.s)
        self.got[self.me()] = self.msg[self.me()]

    def axis(self):
        return "col" if self.t == 0 else "row"

    def me(self):
        return self.s if self.t == 0 else self.r

    def others(self):
        return pl.ds(0, COLS - 1 if self.t == 0 else ROWS - 1)

    def lines_in(self):
        drain(self.got.at[self.others()], self.sems.at[7])
        if self.t == 0:
            for p in range(COLS):
                v = self.got[p].astype(F32)
                for u in range(3):
                    self.line[pl.ds(u * NRES + p * JL, JL), :] = v[u * JL:(u + 1) * JL]
        else:
            for p in range(ROWS):
                for u in range(3):
                    self.line[pl.ds(u * NRES + p * IL, IL), :] = self.got[p, u * IL:(u + 1) * IL, :].astype(F32)

    def lay(self, a):
        drain(self.p1.at[pl.ds(0, ROWS - 1), three(a)], self.sems.at[4 + a])
        v = [jnp.concatenate([self.p1[p, 3 * a + i] for i in range(3)], axis=1) for p in range(ROWS)]
        for b in range(8):
            row = jnp.concatenate([u[:, IL * b:IL * (b + 1)] for u in v], axis=1)
            for i in range(3):
                self.bias[pl.ds(self.s * HEADS * STRIP + i * JL + 8 * a + b, HEADS, stride=STRIP), :] = row[:, 128 * i:128 * (i + 1)]

    def project(self, u):
        rows = pl.ds(u * NRES, NRES)
        p = dot(self.line[rows, :].astype(BF16), self.w_project[self.t])
        self.qs[rows, :] = p[:, :CZ].astype(BF16)
        self.ks[rows, :] = p[:, CZ:2 * CZ].astype(BF16)
        v = p[:, 2 * CZ:3 * CZ]
        if self.t == 0:
            self.vt[pl.ds(u * CZ, CZ), :] = v.T.astype(BF16)
        else:
            self.vs[rows, :] = v.astype(BF16)
        self.gs[rows, :] = jax.nn.sigmoid(p[:, 3 * CZ:])

    def weights_of(self, scores, bias):
        e = scores * (SCALE * LOG2E) + bias
        return jnp.exp2(e - jnp.max(e, axis=self.t, keepdims=True))

    def bias_rows(self, slot, h, i):
        return self.bias[pl.ds(pl.multiple_of((slot * HEADS + h) * STRIP + i * JL, 8), JL), :]

    def tile(self, u, h):
        keep = lax.broadcasted_iota(jnp.int32, (1, CZ), 1) // DH == h
        k = self.ks[pl.ds(u * NRES, NRES), :]
        if self.t == 0:
            vt = self.vt[pl.ds(pl.multiple_of(u * CZ + h * DH, DH), DH), :]
            for i in range(3):
                q = self.qs[pl.ds(u * NRES + i * 128, 128), :]
                q = jnp.where(keep, q, jnp.zeros_like(q))
                b = jnp.concatenate([self.bias_rows(p, h, i) for p in range(COLS)], axis=0)
                e = self.weights_of(dot(k, q, ((1,), (1,))), b)
                o = dot(vt, e.astype(BF16)) / jnp.sum(e, axis=0, keepdims=True)
                self.ot[pl.ds(pl.multiple_of(u * CZ + h * DH, DH), DH), pl.ds(i * 128, 128)] = o
        else:
            v = self.vs[pl.ds(u * NRES, NRES), :]
            k = jnp.where(keep, k, jnp.zeros_like(k))
            v = jnp.concatenate([jnp.where(keep, v, jnp.zeros_like(v)), jnp.ones_like(v)], axis=1)
            for i in range(4):
                rows = pl.ds(u * NRES + i * 96, 96)
                b = jnp.concatenate([
                    jnp.concatenate([self.bias_rows(4 * i + p, h, w) for p in range(4)], axis=0) for w in range(3)], axis=1)
                e = self.weights_of(dot(self.qs[rows, :], k, ((1,), (1,))), b)
                o = dot(e.astype(BF16), v)
                o = o[:, :CZ] / o[:, CZ:]
                self.acc[rows, :] = self.acc[rows, :] + o

    def merge(self, u):
        rows = pl.ds(u * NRES, NRES)
        att = self.ot[pl.ds(u * CZ, CZ), :].T if self.t == 0 else self.acc[rows, :]
        self.us[rows, :] = dot((self.gs[rows, :] * att).astype(BF16), self.w_out[self.t])

    def run(self):
        self.lines_out()
        repeat(PARTS, self.lay)
        repeat(HEADS, lambda h: self.pass_on((0, 0, 0), h, (1, 0, 0), (0, 1, 0), (0, 3, 0), (0, 0, 1)))
        self.lines_in()
        if self.t == 1:
            self.acc[...] = jnp.zeros_like(self.acc)
        for u in range(3):
            self.project(u)

        def head(turn):
            for step in range(3):
                h = turn - step
                pl.when((h >= 0) & (h < HEADS))(lambda: self.forward(h, step))

            @pl.when(turn >= 3)
            def _():
                self.forward(turn - 3, 3)
                for u in range(3):
                    self.tile(u, turn - 3)

        repeat(HEADS + 3, head)
        for u in range(3):
            self.merge(u)
        if self.t == 0:
            for p in range(COLS):
                v = [self.us[pl.ds(u * NRES + p * JL, JL), :] for u in range(3)]
                self.upd[p] = jnp.concatenate(v + [jnp.zeros((LINE0 - 72, CZ), F32)], axis=0).astype(BF16)
        else:
            for p in range(ROWS):
                for u in range(3):
                    self.upd[p, u * IL:(u + 1) * IL, :] = self.us[pl.ds(u * NRES + p * IL, IL), :].astype(BF16)
        scatter_to(self.axis(), lambda p: self.upd.at[p], self.back.at[self.me()], self.sems.at[3], self.sems.at[8], self.r, self.s)
        self.back[self.me()] = self.upd[self.me()]
        drain(self.back.at[self.others()], self.sems.at[8])
        if self.t == 0:
            for p in range(COLS):
                v = self.back[p].astype(F32)
                for u in range(3):
                    rows = pl.ds(3 * p + u, JL, stride=IL)
                    self.x[rows, :] = self.x[rows, :] + v[u * JL:(u + 1) * JL]
        else:
            for p in range(ROWS):
                rows = pl.ds(p * 3 * IL, 3 * IL)
                self.x[rows, :] = self.x[rows, :] + self.back[p].astype(F32)

    def close(self):
        drain(self.p1.at[pl.ds(0, ROWS - 1)], self.sems.at[0])
        drain(self.msg.at[self.others()], self.sems.at[1])
        drain(self.bias.at[pl.ds(0, 15 * HEADS * STRIP)], self.sems.at[2])
        drain(self.upd.at[self.others()], self.sems.at[3])


def kernel(pair, chain, live, table, proj, gate, out, att_w, bias_w, att_o, y, x, nb, mask, kb, stage, left, right, *more):
    r = lax.axis_index("row")
    s = lax.axis_index("col")
    barrier = pltpu.get_barrier_semaphore()
    for axis in ("row", "col"):
        to_peers(axis, r, s, lambda _, device: pl.semaphore_signal(barrier, inc=1, device_id=device, device_id_type=MESH))

    first, second = (r * IL).astype(F32), (s * JL).astype(F32)
    live_count = jnp.sum(live[...].astype(F32), axis=1, keepdims=True)
    begins = [jnp.sum((chain[...] < c).astype(F32), axis=1, keepdims=True) for c in (1, 2, 3)]

    def chain_of(residue):
        return sum((residue >= b).astype(F32) for b in begins)

    px = (lax.broadcasted_iota(jnp.int32, (QS, 128), 0) * 128 + lax.broadcasted_iota(jnp.int32, (QS, 128), 1)).astype(F32)
    jl = jnp.floor((px + 0.5) * (1.0 / IL))
    live_i = (first + px - IL * jl < live_count).astype(F32)
    live_j = (second + jl < live_count).astype(F32)
    mask[...] = live_i * live_j
    kb[0] = (live_j - 1.0) * 1e9
    kb[1] = (live_i - 1.0) * 1e9
    chain_i = chain_of(first + lax.broadcasted_iota(jnp.int32, (IL, CZ), 0).astype(F32))
    for j in range(JL):
        same = chain_i == chain_of(second + jnp.full((1, CZ), j, F32))
        x[pl.ds(j * IL, IL), :] = pair[pl.ds(j, IL, stride=JL), :] + jnp.where(same, table[1:2, :], table[0:1, :])

    more = list(more)

    def take(n):
        got, more[:] = more[:n], more[n:]
        return got

    tri_bufs = [take(8), take(8)]
    att_bufs = [take(6), take(6)]
    shared = take(len(Attention.SHARED))
    tri_send, tri_recv, att_sems, slots = take(4)
    tri = [Triangle(t, x, nb, mask, (proj, gate, out), tri_bufs[t], stage, left, right, tri_send.at[t], tri_recv.at[t], r, s) for t in range(2)]
    att = [Attention(t, x, kb, (bias_w, att_w, att_o), att_bufs[t], shared, att_sems.at[t], slots.at[t], r, s) for t in range(2)]

    pl.semaphore_wait(barrier, ROWS + COLS - 2)
    repeat(PARTS, tri[0].side)
    tri[0].middle()
    repeat(PARTS, lambda a: (tri[0].finish(a), tri[1].side(a)))
    tri[1].middle()
    repeat(PARTS, lambda a: (tri[1].finish(a), att[0].chunk(a)))
    att[0].run()
    repeat(PARTS, att[1].chunk)
    att[1].run()
    for j in range(JL):
        y[pl.ds(j, IL, stride=JL), :] = x[pl.ds(j * IL, IL), :]
    for part in tri + att:
        part.close()


def call(*args):
    vm = pl.BlockSpec(memory_space=pltpu.VMEM)
    shapes = [
        ((PX, CZ), F32), ((PX, CZ), BF16), ((QS, 128), F32), ((2, QS, 128), F32), ((3 * 256, 128), F32), ((3 * NRES, 128), F32),
        ((3 * NRES, 128), F32), *Triangle.SHAPES, *Triangle.SHAPES, *Attention.shapes(0), *Attention.shapes(1), *Attention.SHARED,
    ]
    return pl.pallas_call(
        kernel,
        out_shape=jax.ShapeDtypeStruct((PX, CZ), F32),
        in_specs=[vm] * len(args),
        out_specs=vm,
        scratch_shapes=[pltpu.VMEM(*shape) for shape in shapes] + [
            pltpu.SemaphoreType.DMA((2, 4)),
            pltpu.SemaphoreType.DMA((2, 4, PARTS)),
            pltpu.SemaphoreType.DMA((2, 9)),
            pltpu.SemaphoreType.DMA((2, COLS, HEADS)),
        ],
        compiler_params=pltpu.CompilerParams(collective_id=0, has_side_effects=True, vmem_limit_bytes=56 << 20),
    )(*args)


def local(pair_rep, chain_id, live_mask, chain_table, tri_proj, tri_gate, tri_out, att_project, att_bias, att_out):
    bias_w = jnp.pad(jnp.swapaxes(att_bias, 1, 2), ((0, 0), (0, 8 - HEADS), (0, 0)))
    pair_out = call(
        pair_rep.reshape(PX, CZ), chain_id.reshape(1, NRES), live_mask.reshape(1, NRES), chain_table, tri_proj, tri_gate, tri_out,
        att_project, bias_w, att_out,
    )
    return pair_out.reshape(pair_rep.shape)


def solution(mesh):
    return jax.shard_map(
        local,
        mesh=mesh,
        in_specs=(P("row", "col", None), P(), P(), P(), P(), P(), P(), P(), P(), P()),
        out_specs=P("row", "col", None),
        check_vma=False,
    )
```

time: 995 us -> 152 us (0.15)
  waiting for transfers between devices: 765 us -> 0 us
  Pallas kernels: 0 us -> 147 us
  local copies, waits for them, and re-layouts: 84.1 us -> 4.34 us
  matrix products: 60.6 us -> 0 us
  blocking collectives: 27.4 us -> 0 us
  other arithmetic: 22.8 us -> 0 us
  between operations: 14.4 us -> 0.01 us
  starting transfers between devices: 10.6 us -> 0 us
    all_gather x6 -> x0, waiting for transfers between devices: 545 us -> none  [the longest x2 366 us: full_bias(): gathered = lax.all_gather(tile_bias, ('row', 'col'), axis=0, tiled=True)]
    psum x2 -> x0, waiting for transfers between devices: 203 us -> none  [broadcast(): return lax.psum(block, axis)]
    pallas_call x0 -> x1, Pallas kernels: none -> 147 us  [call(): pl.pallas_call(kernel, out_shape=jax.ShapeDtypeStruct((PX, CZ), F32), in_...]
    dot_general x23 -> x0, matrix products: 47 us -> none  [the longest x8 20.4 us: one_head(): jnp.einsum('ijk,ikd->ijd', weight, values_head, preferred_element_type=jn...]
    all_gather x3 -> x0, local copies, waits for them, and re-layouts: 29.6 us -> none  [the longest x1 22.1 us: local(): lax.all_gather(left_side, 'col', axis=1, tiled=True)]
    all_to_all x2 -> x0, blocking collectives: 27.4 us -> none  [the longest x1 14.4 us: local(): lax.all_to_all(update, 'row', split_axis=0, concat_axis=1, tiled=True)]
    reshape x6 -> x2, local copies, waits for them, and re-layouts: 19.6 us -> 1.13 us  [the longest x1 0.59 us: local(): chain_id.reshape(1, NRES)]
    all_to_all x2 -> x0, waiting for transfers between devices: 16.3 us -> none  [the longest x1 8.88 us: local(): lax.all_to_all(normed.astype(jnp.bfloat16), 'row', split_axis=1, concat_a...]
  transfers between devices with their start and end apart: 10 -> 0, of which waited for: 10 -> 0; matrix products, arithmetic and copies ran while one was open for 4% -> 0% of each run, Pallas kernels for 0% -> 0%
where the time goes in v3:
time: 152 us
  Pallas kernels  147 us (97%)
  local copies, waits for them, and re-layouts  4.34 us (3%)
    pallas_call x1, Pallas kernels, call(): pl.pallas_call(kernel, out_shape=jax.ShapeDtypeStruct((PX, CZ), F32), in_...  147 us

profile of v3, /device:TPU:0, one launch (start us, length us, event | category | flops | bytes accessed | tf_op | source)
XLA Modules:
  0.0 151.7 jit_solution(1330947914415692187)
XLA Ops:
  0.0 0.0 copy-start.1
  0.0 0.0 copy-start.2
  0.0 0.0 copy-start
  0.0 0.7 copy-done.1
  0.7 0.6 reshape.13.chain
  1.3 0.0 copy-done.2
  1.3 0.5 reshape.14.live
  1.8 0.0 copy-done
  1.8 0.6 pad.4.bias_w
  2.4 147.4 %shard_map.100 = f32[1152,128]{1,0:T(8,128)} custom-call(f32[1152,128]{1,0:T(8,128)} %bitcast.4, s32[1,384]{1,0:T(1,128)} %reshape.13.chain, s32[1,384]{1,0:T(1,128)} %reshape.14.live, f32[2,128]{1,0:T(2,128)} %table.1, bf16[2,128,512]{2,1,0:T(8,128)(2,1)} %proj.1, bf16[2,128,128]{2,1,0:T(8,128)(2,1)} %gate.1, bf16[2,128,128]{2,1,0:T(8,128)(2,1)} %out.1, ...), custom_call_target="tpu_custom_call" | custom-call | tf_op jit(solution)/shard_map/pallas_call | solution.py:465
  149.8 1.9 %copy.12 = f32[48,24,128]{2,1,0:T(8,128)} copy(f32[48,24,128]{2,1,0:T(8,128)} %bitcast.3) | data formatting | bytes 1179648
Async XLA Ops:
  0.0 0.7 copy-start.1
  0.0 1.3 copy-start.2
  0.0 1.8 %copy-start = (f32[2,128,4]{1,2,0:T(4,128)S(1)}, f32[2,128,4]{1,2,0:T(4,128)}, u32[]{:S(2)}) copy-start(f32[2,128,4]{1,2,0:T(4,128)} %param.18) | copy-start | bytes 12292

commit v4 on v3

--- a/solution.py
+++ b/solution.py
@@ -45,7 +45,7 @@
     n, me = (ROWS, r) if axis == "row" else (COLS, s)
 
     def one(d):
-        p = jnp.bitwise_xor(me, d)
+        p = jnp.bitwise_xor(me, n - d)
         act(p, (p, s) if axis == "row" else (r, p))
 
     repeat(n, one, 1)
@@ -80,7 +80,6 @@
         self.stage, self.left, self.right, self.sends, self.recvs = stage, left, right, sends, recvs
 
     def side(self, a):
-        r, s = self.r, self.s
 
         def chunk(i, _):
             q = 3 * a + i
@@ -97,6 +96,9 @@
             return 0
 
         lax.fori_loop(0, 3, chunk, 0)
+
+    def side_out(self, a):
+        r, s = self.r, self.s
         scatter_to("row", lambda p: self.s1.at[p, three(a)], self.r1.at[r, three(a)], self.sends.at[0], self.recvs.at[0, a], r, s)
         self.r1[r, three(a)] = self.s1[r, three(a)]
 
@@ -402,7 +404,7 @@
         drain(self.upd.at[self.others()], self.sems.at[3])
 
 
-def kernel(pair, chain, live, table, proj, gate, out, att_w, bias_w, att_o, y, x, nb, mask, kb, stage, left, right, *more):
+def kernel(pair, chain, live, table, proj, gate, out, att_w, bias_c, att_o, y, x, nb, mask, kb, bias_w, stage, left, right, *more):
     r = lax.axis_index("row")
     s = lax.axis_index("col")
     barrier = pltpu.get_barrier_semaphore()
@@ -410,8 +412,8 @@
         to_peers(axis, r, s, lambda _, device: pl.semaphore_signal(barrier, inc=1, device_id=device, device_id_type=MESH))
 
     first, second = (r * IL).astype(F32), (s * JL).astype(F32)
-    live_count = jnp.sum(live[...].astype(F32), axis=1, keepdims=True)
-    begins = [jnp.sum((chain[...] < c).astype(F32), axis=1, keepdims=True) for c in (1, 2, 3)]
+    live_count = jnp.sum(live[...].reshape(1, NRES).astype(F32), axis=1, keepdims=True)
+    begins = [jnp.sum((chain[...].reshape(1, NRES) < c).astype(F32), axis=1, keepdims=True) for c in (1, 2, 3)]
 
     def chain_of(residue):
         return sum((residue >= b).astype(F32) for b in begins)
@@ -423,6 +425,9 @@
     mask[...] = live_i * live_j
     kb[0] = (live_j - 1.0) * 1e9
     kb[1] = (live_i - 1.0) * 1e9
+    for t in range(2):
+        wide = jnp.concatenate([bias_c[t], jnp.zeros((CZ, 128 - HEADS), F32)], axis=1)
+        bias_w[t] = wide.T[:8]
     chain_i = chain_of(first + lax.broadcasted_iota(jnp.int32, (IL, CZ), 0).astype(F32))
     for j in range(JL):
         same = chain_i == chain_of(second + jnp.full((1, CZ), j, F32))
@@ -441,10 +446,12 @@
     tri = [Triangle(t, x, nb, mask, (proj, gate, out), tri_bufs[t], stage, left, right, tri_send.at[t], tri_recv.at[t], r, s) for t in range(2)]
     att = [Attention(t, x, kb, (bias_w, att_w, att_o), att_bufs[t], shared, att_sems.at[t], slots.at[t], r, s) for t in range(2)]
 
+    tri[0].side(0)
     pl.semaphore_wait(barrier, ROWS + COLS - 2)
-    repeat(PARTS, tri[0].side)
+    tri[0].side_out(0)
+    repeat(PARTS, lambda a: (tri[0].side(a), tri[0].side_out(a)), 1)
     tri[0].middle()
-    repeat(PARTS, lambda a: (tri[0].finish(a), tri[1].side(a)))
+    repeat(PARTS, lambda a: (tri[0].finish(a), tri[1].side(a), tri[1].side_out(a)))
     tri[1].middle()
     repeat(PARTS, lambda a: (tri[1].finish(a), att[0].chunk(a)))
     att[0].run()
@@ -459,7 +466,7 @@
 def call(*args):
     vm = pl.BlockSpec(memory_space=pltpu.VMEM)
     shapes = [
-        ((PX, CZ), F32), ((PX, CZ), BF16), ((QS, 128), F32), ((2, QS, 128), F32), ((3 * 256, 128), F32), ((3 * NRES, 128), F32),
+        ((PX, CZ), F32), ((PX, CZ), BF16), ((QS, 128), F32), ((2, QS, 128), F32), ((2, 8, CZ), F32), ((3 * 256, 128), F32), ((3 * NRES, 128), F32),
         ((3 * NRES, 128), F32), *Triangle.SHAPES, *Triangle.SHAPES, *Attention.shapes(0), *Attention.shapes(1), *Attention.SHARED,
     ]
     return pl.pallas_call(
@@ -478,10 +485,9 @@
 
 
 def local(pair_rep, chain_id, live_mask, chain_table, tri_proj, tri_gate, tri_out, att_project, att_bias, att_out):
-    bias_w = jnp.pad(jnp.swapaxes(att_bias, 1, 2), ((0, 0), (0, 8 - HEADS), (0, 0)))
     pair_out = call(
-        pair_rep.reshape(PX, CZ), chain_id.reshape(1, NRES), live_mask.reshape(1, NRES), chain_table, tri_proj, tri_gate, tri_out,
-        att_project, bias_w, att_out,
+        pair_rep.reshape(PX, CZ), chain_id, live_mask, chain_table, tri_proj, tri_gate, tri_out,
+        att_project, att_bias, att_out,
     )
     return pair_out.reshape(pair_rep.shape)
 

time: 152 us -> 147 us (0.967)
  Pallas kernels: 147 us -> 143 us
    pallas_call x1, Pallas kernels: 147 us -> 143 us  [call(): pl.pallas_call(kernel, out_shape=jax.ShapeDtypeStruct((PX, CZ), F32), in_...]
    unnamed x7 -> x2, local copies, waits for them, and re-layouts: 2.6 us -> 3.4 us
where the time goes in v4:
time: 147 us
  Pallas kernels  143 us (97%)
  local copies, waits for them, and re-layouts  3.4 us (2%)
    pallas_call x1, Pallas kernels, call(): pl.pallas_call(kernel, out_shape=jax.ShapeDtypeStruct((PX, CZ), F32), in_...  143 us
    unnamed x2, local copies, waits for them, and re-layouts  3.4 us

profile of v4, /device:TPU:0, one launch (start us, length us, event | category | flops | bytes accessed | tf_op | source)
XLA Modules:
  0.0 146.9 jit_solution(7305318386976854430)
XLA Ops:
  0.0 1.5 %copy.11.bias_c = f32[2,128,4]{2,1,0:T(8,128)} copy(f32[2,128,4]{1,2,0:T(4,128)} %param.18) | data formatting | bytes 8192 | tf_op args[8]
  1.5 143.5 %shard_map.100 = f32[1152,128]{1,0:T(8,128)} custom-call(f32[1152,128]{1,0:T(8,128)} %bitcast.3, s32[384]{0:T(512)} %chain.1, s32[384]{0:T(512)} %live.1, f32[2,128]{1,0:T(2,128)} %table.1, bf16[2,128,512]{2,1,0:T(8,128)(2,1)} %proj.1, bf16[2,128,128]{2,1,0:T(8,128)(2,1)} %gate.1, bf16[2,128,128]{2,1,0:T(8,128)(2,1)} %out.1, bf16[2,128,512]{2,1,0:T(8,128)(2,1)} %att_w.1, ...), custom_call_target="tpu_custom_call" | custom-call | tf_op jit(solution)/shard_map/pallas_call | solution.py:472
  145.0 1.9 %copy.13 = f32[48,24,128]{2,1,0:T(8,128)} copy(f32[48,24,128]{2,1,0:T(8,128)} %bitcast.2) | data formatting | bytes 1179648

commit v5 on v4

--- a/solution.py
+++ b/solution.py
@@ -29,6 +29,10 @@
     return c * lax.rsqrt(spread + 1e-05)
 
 
+def sigmoid(v):
+    return 0.5 * jnp.tanh(0.5 * v) + 0.5
+
+
 def dot(a, b, dims=((1,), (0,))):
     return lax.dot_general(a, b, (dims, ((), ())), preferred_element_type=F32)
 
@@ -89,7 +93,7 @@
             p = dot(n, self.proj[self.t])
             m = self.mask[pl.ds(q, 1), :]
             for k in range(2):
-                v = jax.nn.sigmoid(p[:, (2 * k + 1) * CZ:(2 * k + 2) * CZ]) * p[:, 2 * k * CZ:(2 * k + 1) * CZ]
+                v = sigmoid(p[:, (2 * k + 1) * CZ:(2 * k + 2) * CZ]) * p[:, 2 * k * CZ:(2 * k + 1) * CZ]
                 v = (v.T * m).astype(BF16)
                 for p_ in range(ROWS):
                     self.s1[p_, q, 16 * k:16 * k + 16, :] = v[16 * p_:16 * p_ + 16]
@@ -168,7 +172,7 @@
             rows = pl.ds(pl.multiple_of(q * 128, 128), 128)
             pr = jnp.concatenate([self.r4[p, q] for p in range(ROWS)], axis=0).astype(F32).T
             mixed = normalize(pr).astype(BF16)
-            g = jax.nn.sigmoid(dot(self.nb[rows, :], self.gate[self.t]))
+            g = sigmoid(dot(self.nb[rows, :], self.gate[self.t]))
             self.x[rows, :] = self.x[rows, :] + g * dot(mixed, self.out[self.t])
             return 0
 
@@ -242,14 +246,14 @@
     def forward(self, h, step):
         across, up, down, other = (1, 0, 0), (0, 1, 0), (0, 3, 0), (0, 0, 1)
         if step == 0:
-            self.arrived(across, h)
-            self.pass_on(across, h, up, down, other)
             self.arrived(up, h)
             self.pass_on(up, h, other)
             self.arrived(down, h)
             self.pass_on(down, h, other)
             pl.when(h < 2)(lambda: self.pass_on(up, h, down))
             pl.when(h >= 2)(lambda: self.pass_on(down, h, up))
+            self.arrived(across, h)
+            self.pass_on(across, h, up, down, other)
         elif step == 1:
             self.arrived((0, 2, 0), h)
             self.pass_on((0, 2, 0), h, across, other)
@@ -312,7 +316,7 @@
             self.vt[pl.ds(u * CZ, CZ), :] = v.T.astype(BF16)
         else:
             self.vs[rows, :] = v.astype(BF16)
-        self.gs[rows, :] = jax.nn.sigmoid(p[:, 3 * CZ:])
+        self.gs[rows, :] = sigmoid(p[:, 3 * CZ:])
 
     def weights_of(self, scores, bias):
         e = scores * (SCALE * LOG2E) + bias
@@ -354,7 +358,7 @@
     def run(self):
         self.lines_out()
         repeat(PARTS, self.lay)
-        repeat(HEADS, lambda h: self.pass_on((0, 0, 0), h, (1, 0, 0), (0, 1, 0), (0, 3, 0), (0, 0, 1)))
+        repeat(HEADS, lambda h: self.pass_on((0, 0, 0), h, (0, 1, 0), (0, 3, 0), (1, 0, 0), (0, 0, 1)))
         self.lines_in()
         if self.t == 1:
             self.acc[...] = jnp.zeros_like(self.acc)

time: 147 us -> 147 us (level)
  no operation moved by 1% of the time
where the time goes in v5:
time: 147 us; the launch traced here: 146 us
  Pallas kernels  143 us (97%)
  local copies, waits for them, and re-layouts  3.4 us (2%)
    pallas_call x1, Pallas kernels, call(): pl.pallas_call(kernel, out_shape=jax.ShapeDtypeStruct((PX, CZ), F32), in_...  143 us
    unnamed x2, local copies, waits for them, and re-layouts  3.4 us

profile of v5, /device:TPU:0, one launch (start us, length us, event | category | flops | bytes accessed | tf_op | source)
XLA Modules:
  0.0 146.3 jit_solution(4865597495312705278)
XLA Ops:
  0.0 1.5 %copy.11.bias_c = f32[2,128,4]{2,1,0:T(8,128)} copy(f32[2,128,4]{1,2,0:T(4,128)} %param.18) | data formatting | bytes 8192 | tf_op args[8]
  1.5 142.9 %shard_map.100 = f32[1152,128]{1,0:T(8,128)} custom-call(f32[1152,128]{1,0:T(8,128)} %bitcast.3, s32[384]{0:T(512)} %chain.1, s32[384]{0:T(512)} %live.1, f32[2,128]{1,0:T(2,128)} %table.1, bf16[2,128,512]{2,1,0:T(8,128)(2,1)} %proj.1, bf16[2,128,128]{2,1,0:T(8,128)(2,1)} %gate.1, bf16[2,128,128]{2,1,0:T(8,128)(2,1)} %out.1, bf16[2,128,512]{2,1,0:T(8,128)(2,1)} %att_w.1, ...), custom_call_target="tpu_custom_call" | custom-call | tf_op jit(solution)/shard_map/pallas_call | solution.py:476
  144.4 1.9 %copy.13 = f32[48,24,128]{2,1,0:T(8,128)} copy(f32[48,24,128]{2,1,0:T(8,128)} %bitcast.2) | data formatting | bytes 1179648

commit v6 on v5

--- a/solution.py
+++ b/solution.py
@@ -37,12 +37,12 @@
     return lax.dot_general(a, b, (dims, ((), ())), preferred_element_type=F32)
 
 
-def repeat(n, body, first=0):
+def repeat(n, body, first=0, unroll=1):
     def step(i, carry):
         body(i)
         return carry
 
-    lax.fori_loop(first, n, step, 0)
+    lax.fori_loop(first, n, step, 0, unroll=unroll)
 
 
 def to_peers(axis, r, s, act):
@@ -52,7 +52,7 @@
         p = jnp.bitwise_xor(me, n - d)
         act(p, (p, s) if axis == "row" else (r, p))
 
-    repeat(n, one, 1)
+    repeat(n, one, 1, 7 if n == ROWS else 5)
 
 
 def scatter_to(axis, src, dst, send, recv, r, s):

time: 147 us -> 146 us (level)
  no operation moved by 1% of the time
where the time goes in v6:
time: 146 us
  Pallas kernels  142 us (97%)
  local copies, waits for them, and re-layouts  3.4 us (2%)
    pallas_call x1, Pallas kernels, call(): pl.pallas_call(kernel, out_shape=jax.ShapeDtypeStruct((PX, CZ), F32), in_...  142 us
    unnamed x2, local copies, waits for them, and re-layouts  3.4 us

profile of v6, /device:TPU:0, one launch (start us, length us, event | category | flops | bytes accessed | tf_op | source)
XLA Modules:
  0.0 145.9 jit_solution(8471129115906278028)
XLA Ops:
  0.0 1.5 %copy.11.bias_c = f32[2,128,4]{2,1,0:T(8,128)} copy(f32[2,128,4]{1,2,0:T(4,128)} %param.18) | data formatting | bytes 8192 | tf_op args[8]
  1.5 142.5 %shard_map.100 = f32[1152,128]{1,0:T(8,128)} custom-call(f32[1152,128]{1,0:T(8,128)} %bitcast.3, s32[384]{0:T(512)} %chain.1, s32[384]{0:T(512)} %live.1, f32[2,128]{1,0:T(2,128)} %table.1, bf16[2,128,512]{2,1,0:T(8,128)(2,1)} %proj.1, bf16[2,128,128]{2,1,0:T(8,128)(2,1)} %gate.1, bf16[2,128,128]{2,1,0:T(8,128)(2,1)} %out.1, bf16[2,128,512]{2,1,0:T(8,128)(2,1)} %att_w.1, ...), custom_call_target="tpu_custom_call" | custom-call | tf_op jit(solution)/shard_map/pallas_call | solution.py:476
  144.0 1.9 %copy.13 = f32[48,24,128]{2,1,0:T(8,128)} copy(f32[48,24,128]{2,1,0:T(8,128)} %bitcast.2) | data formatting | bytes 1179648

commit v7 on v6

--- a/solution.py
+++ b/solution.py
@@ -99,7 +99,7 @@
                     self.s1[p_, q, 16 * k:16 * k + 16, :] = v[16 * p_:16 * p_ + 16]
             return 0
 
-        lax.fori_loop(0, 3, chunk, 0)
+        lax.fori_loop(0, 3, chunk, 0, unroll=3)
 
     def side_out(self, a):
         r, s = self.r, self.s
@@ -120,7 +120,7 @@
                 self.s2[c, q] = mid[pl.ds(pl.multiple_of(i * 256 + c * 16, 16), 16), :].astype(BF16)
             return 0
 
-        lax.fori_loop(0, 3, chunk, 0)
+        lax.fori_loop(0, 3, chunk, 0, unroll=3)
         scatter_to("col", lambda p: self.s2.at[p, three(a)], self.r2.at[s, three(a)], self.sends.at[1], self.recvs.at[1, a], r, s)
         self.r2[s, three(a)] = self.s2[s, three(a)]
 
@@ -176,7 +176,7 @@
             self.x[rows, :] = self.x[rows, :] + g * dot(mixed, self.out[self.t])
             return 0
 
-        lax.fori_loop(0, 3, chunk, 0)
+        lax.fori_loop(0, 3, chunk, 0, unroll=3)
 
     def middle(self):
         for step in (self.relay, self.gather):
@@ -221,7 +221,7 @@
             self.p1[r, q] = (b8[:HEADS] + self.kb[t, pl.ds(q, 1), :]) * LOG2E
             return 0
 
-        lax.fori_loop(0, 3, one, 0)
+        lax.fori_loop(0, 3, one, 0, unroll=3)
         mine = self.p1.at[r, three(a)]
         scatter_to("row", lambda p: mine, mine, self.sems.at[0], self.sems.at[4 + a], r, s)
 

time: 146 us -> 139 us (0.952)
  Pallas kernels: 142 us -> 136 us
    pallas_call x1, Pallas kernels: 142 us -> 136 us  [call(): pl.pallas_call(kernel, out_shape=jax.ShapeDtypeStruct((PX, CZ), F32), in_...]
where the time goes in v7:
time: 139 us
  Pallas kernels  136 us (98%)
  local copies, waits for them, and re-layouts  3.4 us (2%)
    pallas_call x1, Pallas kernels, call(): pl.pallas_call(kernel, out_shape=jax.ShapeDtypeStruct((PX, CZ), F32), in_...  136 us
    unnamed x2, local copies, waits for them, and re-layouts  3.4 us

profile of v7, /device:TPU:0, one launch (start us, length us, event | category | flops | bytes accessed | tf_op | source)
XLA Modules:
  0.0 139.2 jit_solution(12835236761664482303)
XLA Ops:
  0.0 1.5 %copy.11.bias_c = f32[2,128,4]{2,1,0:T(8,128)} copy(f32[2,128,4]{1,2,0:T(4,128)} %param.18) | data formatting | bytes 8192 | tf_op args[8]
  1.5 135.8 %shard_map.100 = f32[1152,128]{1,0:T(8,128)} custom-call(f32[1152,128]{1,0:T(8,128)} %bitcast.3, s32[384]{0:T(512)} %chain.1, s32[384]{0:T(512)} %live.1, f32[2,128]{1,0:T(2,128)} %table.1, bf16[2,128,512]{2,1,0:T(8,128)(2,1)} %proj.1, bf16[2,128,128]{2,1,0:T(8,128)(2,1)} %gate.1, bf16[2,128,128]{2,1,0:T(8,128)(2,1)} %out.1, bf16[2,128,512]{2,1,0:T(8,128)(2,1)} %att_w.1, ...), custom_call_target="tpu_custom_call" | custom-call | tf_op jit(solution)/shard_map/pallas_call | solution.py:476
  137.3 1.9 %copy.13 = f32[48,24,128]{2,1,0:T(8,128)} copy(f32[48,24,128]{2,1,0:T(8,128)} %bitcast.2) | data formatting | bytes 1179648
